TPU v7x, 32 devices: a whole 2x2x4 slice. The times are simulated.
32 devices in a mesh: dp: 4 (over x, core), fsdp: 2 (over y), mp: 4 (over z).
Axes of the slice: x: 2, y: 2, z: 4, core: 2. Of those that a mesh axis runs over, the one named last changes fastest.
Arguments:
- inputs: bfloat16 [5120, 1536], P(('dp', 'fsdp', 'mp')), may hold values from -6 to 6
- clip_ids: int32 [5120], P(('dp', 'fsdp')), may hold values from 0 to 3, as said below
- clip_pos: int32 [5120], P(('dp', 'fsdp')), may hold values from 0 to 1535, as said below
- text_states: bfloat16 [4, 64, 1536], replicated, may hold values from -6 to 6
- norm_gain: bfloat16 [2, 3, 1536], P(None, None, 'fsdp'), may hold values from 0.099609375 to 1.8984375
- norm_bias: bfloat16 [2, 3, 1536], P(None, None, 'fsdp'), may hold values from -1.5 to 1.5
- self_qkv: bfloat16 [2, 1536, 3, 1536], P(None, 'fsdp', None, 'mp'), may hold values from -0.15625 to 0.15625
- self_out: bfloat16 [2, 1536, 1536], P(None, 'mp', 'fsdp'), may hold values from -0.625 to 0.625
- cross_q: bfloat16 [2, 1536, 1536], P(None, 'fsdp', 'mp'), may hold values from -0.15625 to 0.15625
- cross_kv: bfloat16 [2, 1536, 2, 1536], P(None, 'fsdp', None, 'mp'), may hold values from -0.15625 to 0.15625
- cross_out: bfloat16 [2, 1536, 1536], P(None, 'mp', 'fsdp'), may hold values from -0.3125 to 0.3125
- mlp_up: bfloat16 [2, 1536, 6144], P(None, 'fsdp', 'mp'), may hold values from -0.15625 to 0.15625
- mlp_down: bfloat16 [2, 6144, 1536], P(None, 'mp', 'fsdp'), may hold values from -0.109375 to 0.109375
- cotangent: bfloat16 [5120, 1536], P(('dp', 'fsdp', 'mp')), may hold values from -6 to 6
Outputs:
- output: bfloat16 [5120, 1536], P(('dp', 'fsdp', 'mp'))
- input_grad: float32 [5120, 1536], P(('dp', 'fsdp', 'mp'))
- text_grad: float32 [4, 64, 1536], replicated
- gain_grad: float32 [2, 3, 1536], P(None, None, 'fsdp')
- bias_grad: float32 [2, 3, 1536], P(None, None, 'fsdp')
- self_qkv_grad: float32 [2, 1536, 3, 1536], P(None, 'fsdp', None, 'mp')
- self_out_grad: float32 [2, 1536, 1536], P(None, 'mp', 'fsdp')
- cross_q_grad: float32 [2, 1536, 1536], P(None, 'fsdp', 'mp')
- cross_kv_grad: float32 [2, 1536, 2, 1536], P(None, 'fsdp', None, 'mp')
- cross_out_grad: float32 [2, 1536, 1536], P(None, 'mp', 'fsdp')
- mlp_up_grad: float32 [2, 1536, 6144], P(None, 'fsdp', 'mp')
- mlp_down_grad: float32 [2, 6144, 1536], P(None, 'mp', 'fsdp')
Inputs may be any that keep to these rules, and one draw needn't show every extreme that they name: `clip_ids`: clip numbers never fall along the stream; every clip has 1024 to 1536 frames, one has exactly 1536 and one exactly 1024; clip k's text states are text_states[k]. clip_pos counts from 0 at the first frame of each clip and rises by one a frame within it.
All inputs are finite; a program needn't handle non-finite values.
Results may differ from a plain program's by a relative error of at most 0.03.
Values may be sent and summed in bfloat16 or wider, within the bound.
No kernel may reach another device: no remote copies, remote signals or barrier semaphores. Data moves between devices by JAX's collectives and lax.ppermute only.
A program may use at most 256 MiB of HBM per device.

v0:
```python
import jax
import jax.numpy as jnp
from jax import lax
from jax.sharding import PartitionSpec as P

HEAD_DIM = 64
TEXT = 64
SLOTS = 2
REACH = 3


norm_eps = 1e-05
score_scale = 0.125
masked_fill = -1e30


def passed_along(value, axis, steps):
    count = lax.axis_size(axis)
    leading, last = (max(0, -steps), min(count, count - steps))
    return lax.ppermute(value, axis, [(source, source + steps) for source in range(leading, last)])


def layer_norm(values, gain_vec, bias_vec):
    center = values - jnp.mean(values, axis=-1, keepdims=True)
    spread = jnp.mean(center * center, axis=-1, keepdims=True)
    return center * lax.rsqrt(spread + norm_eps) * gain_vec + bias_vec


def split_heads(matrix):
    return matrix.reshape(matrix.shape[0], -1, HEAD_DIM).transpose(1, 0, 2)


def merge_heads(stacked):
    return stacked.transpose(1, 0, 2).reshape(stacked.shape[1], -1)


def attend_head(queries_in, keys_in, values_in, allowed):
    scores = (
        jnp.einsum("qe,ke->qk", queries_in, keys_in, preferred_element_type=jnp.float32)
        * score_scale
    )
    scores = jnp.where(allowed, scores, masked_fill)
    top_score = jnp.max(scores, axis=1, keepdims=True)
    expanded = jnp.exp(scores - top_score)
    total_sum = jnp.sum(expanded, axis=1, keepdims=True)
    probs = (expanded / total_sum).astype(jnp.bfloat16)
    result = jnp.einsum("qk,ke->qe", probs, values_in, preferred_element_type=jnp.float32)
    return (result, (top_score + jnp.log(total_sum))[:, 0])


def attend(queries_in, keys_in, values_in, allowed):
    return lax.map(
        lambda triple: attend_head(triple[0], triple[1], triple[2], allowed),
        (queries_in, keys_in, values_in),
    )


def attend_back_head(queries_in, keys_in, values_in, log_total, grad_out, allowed):
    scores = (
        jnp.einsum("qe,ke->qk", queries_in, keys_in, preferred_element_type=jnp.float32)
        * score_scale
    )
    scores = jnp.where(allowed, scores, masked_fill)
    probs = jnp.exp(scores - log_total[:, None])
    grad_probs = jnp.einsum("qe,ke->qk", grad_out, values_in, preferred_element_type=jnp.float32)
    inner_sum = jnp.sum(probs * grad_probs, axis=1, keepdims=True)
    grad_scores = (probs * (grad_probs - inner_sum)).astype(jnp.bfloat16)
    grad_values = jnp.einsum(
        "qk,qe->ke", probs.astype(jnp.bfloat16), grad_out, preferred_element_type=jnp.float32
    )
    grad_queries = (
        jnp.einsum("qk,ke->qe", grad_scores, keys_in, preferred_element_type=jnp.float32)
        * score_scale
    )
    grad_keys = (
        jnp.einsum("qk,qe->ke", grad_scores, queries_in, preferred_element_type=jnp.float32)
        * score_scale
    )
    return (grad_queries, grad_keys, grad_values)


def attend_back(queries_in, keys_in, values_in, log_total, grad_out, allowed):
    return lax.map(
        lambda group: attend_back_head(group[0], group[1], group[2], group[3], group[4], allowed),
        (queries_in, keys_in, values_in, log_total, grad_out),
    )


def local(
    inputs,
    clip_ids,
    clip_pos,
    text_states,
    norm_gain,
    norm_bias,
    self_qkv,
    self_out,
    cross_q,
    cross_kv,
    cross_out,
    mlp_up,
    mlp_down,
    cotangent,
):
    tok_count = clip_ids.shape[0]
    layer_count = norm_gain.shape[0]
    clip_count = text_states.shape[0]
    model_width = inputs.shape[1]

    def spread_rows(values):
        return lax.all_gather(values, "mp", axis=0, tiled=True)

    def reduce_rows(values):
        return lax.psum_scatter(
            values.astype(jnp.bfloat16), "mp", scatter_dimension=0, tiled=True
        ).astype(jnp.float32)

    def gather_grads(values):
        return lax.all_gather(values, "mp", axis=0, tiled=True)

    def reduce_grads(values):
        return lax.psum_scatter(
            values.astype(jnp.bfloat16), "mp", scatter_dimension=0, tiled=True
        ).astype(jnp.float32)

    group_base = lax.axis_index(("dp", "fsdp")) * tok_count
    query_pos = group_base + jnp.arange(tok_count, dtype=jnp.int32)
    window_pos = (
        group_base - REACH * tok_count + jnp.arange((REACH + 1) * tok_count, dtype=jnp.int32)
    )
    clip_start = query_pos - clip_pos
    self_mask = (window_pos[None, :] <= query_pos[:, None]) & (
        window_pos[None, :] >= clip_start[:, None]
    )
    slot_first = jnp.minimum(clip_ids[0], clip_count - SLOTS)
    slot_ids = slot_first + jnp.arange(SLOTS * TEXT, dtype=jnp.int32) // TEXT
    cross_mask = clip_ids[:, None] == slot_ids[None, :]
    text_rows = lax.dynamic_slice_in_dim(text_states, slot_first, SLOTS, 0).reshape(
        SLOTS * TEXT, model_width
    )
    residual = inputs.astype(jnp.float32)
    saved = []
    kept_weights = []
    for layer_index in range(layer_count):
        weights = (
            lax.all_gather(norm_gain[layer_index], "fsdp", axis=1, tiled=True),
            lax.all_gather(norm_bias[layer_index], "fsdp", axis=1, tiled=True),
            lax.all_gather(self_qkv[layer_index], "fsdp", axis=0, tiled=True),
            lax.all_gather(self_out[layer_index], "fsdp", axis=1, tiled=True),
            lax.all_gather(cross_q[layer_index], "fsdp", axis=0, tiled=True),
            lax.all_gather(cross_kv[layer_index], "fsdp", axis=0, tiled=True),
            lax.all_gather(cross_out[layer_index], "fsdp", axis=1, tiled=True),
            lax.all_gather(mlp_up[layer_index], "fsdp", axis=0, tiled=True),
            lax.all_gather(mlp_down[layer_index], "fsdp", axis=1, tiled=True),
        )
        kept_weights.append(weights)
        gain_vec = weights[0].astype(jnp.float32)
        bias_vec = weights[1].astype(jnp.float32)
        start_res = residual
        normed_one = layer_norm(residual, gain_vec[0], bias_vec[0]).astype(jnp.bfloat16)
        rows_one = spread_rows(normed_one)
        projected = jnp.einsum(
            "td,dcj->ctj", rows_one, weights[2], preferred_element_type=jnp.float32
        ).astype(jnp.bfloat16)
        queries = projected[0]
        pieces = [projected[1:]]
        for distance in range(1, REACH + 1):
            pieces.insert(0, passed_along(projected[1:], ("dp", "fsdp"), distance))
        keyvals = jnp.concatenate(pieces, axis=1)
        heads_out, log_self = attend(
            split_heads(queries), split_heads(keyvals[0]), split_heads(keyvals[1]), self_mask
        )
        merged_one = merge_heads(heads_out).astype(jnp.bfloat16)
        residual = residual + reduce_rows(
            jnp.dot(merged_one, weights[3], preferred_element_type=jnp.float32)
        )
        mid_res = residual
        normed_two = layer_norm(residual, gain_vec[1], bias_vec[1]).astype(jnp.bfloat16)
        rows_two = spread_rows(normed_two)
        cross_query = jnp.dot(rows_two, weights[4], preferred_element_type=jnp.float32).astype(
            jnp.bfloat16
        )
        text_kv = jnp.einsum(
            "sd,dcj->csj", text_rows, weights[5], preferred_element_type=jnp.float32
        ).astype(jnp.bfloat16)
        cross_heads, log_cross = attend(
            split_heads(cross_query), split_heads(text_kv[0]), split_heads(text_kv[1]), cross_mask
        )
        merged_two = merge_heads(cross_heads).astype(jnp.bfloat16)
        residual = residual + reduce_rows(
            jnp.dot(merged_two, weights[6], preferred_element_type=jnp.float32)
        )
        late_res = residual
        normed_three = layer_norm(residual, gain_vec[2], bias_vec[2]).astype(jnp.bfloat16)
        rows_three = spread_rows(normed_three)
        upward = jnp.dot(rows_three, weights[7], preferred_element_type=jnp.float32)
        activated = jax.nn.gelu(upward).astype(jnp.bfloat16)
        residual = residual + reduce_rows(
            jnp.dot(activated, weights[8], preferred_element_type=jnp.float32)
        )
        saved.append(
            (
                start_res,
                mid_res,
                late_res,
                rows_one,
                queries,
                keyvals,
                log_self,
                merged_one,
                rows_two,
                cross_query,
                text_kv,
                log_cross,
                merged_two,
                rows_three,
                upward,
                activated,
            )
        )
    output = residual.astype(jnp.bfloat16)
    grad_res = cotangent.astype(jnp.float32)
    text_acc = jnp.zeros((SLOTS * TEXT, model_width), jnp.float32)
    matrix_list = []
    gain_list = []
    bias_list = []
    for layer_index in reversed(range(layer_count)):
        weights = (
            lax.all_gather(norm_gain[layer_index], "fsdp", axis=1, tiled=True),
            lax.all_gather(norm_bias[layer_index], "fsdp", axis=1, tiled=True),
            lax.all_gather(self_qkv[layer_index], "fsdp", axis=0, tiled=True),
            lax.all_gather(self_out[layer_index], "fsdp", axis=1, tiled=True),
            lax.all_gather(cross_q[layer_index], "fsdp", axis=0, tiled=True),
            lax.all_gather(cross_kv[layer_index], "fsdp", axis=0, tiled=True),
            lax.all_gather(cross_out[layer_index], "fsdp", axis=1, tiled=True),
            lax.all_gather(mlp_up[layer_index], "fsdp", axis=0, tiled=True),
            lax.all_gather(mlp_down[layer_index], "fsdp", axis=1, tiled=True),
        )
        gain_vec = weights[0].astype(jnp.float32)
        bias_vec = weights[1].astype(jnp.float32)
        (
            start_res,
            mid_res,
            late_res,
            rows_one,
            queries,
            keyvals,
            log_self,
            merged_one,
            rows_two,
            cross_query,
            text_kv,
            log_cross,
            merged_two,
            rows_three,
            upward,
            activated,
        ) = saved[layer_index]
        grad_full = gather_grads(grad_res.astype(jnp.bfloat16))
        grad_down = jnp.einsum(
            "tf,td->fd", activated, grad_full, preferred_element_type=jnp.float32
        )
        grad_act = jnp.einsum(
            "td,fd->tf", grad_full, weights[8], preferred_element_type=jnp.float32
        )
        grad_upward = jax.vjp(jax.nn.gelu, upward)[1](grad_act)[0].astype(jnp.bfloat16)
        grad_up = jnp.einsum(
            "td,tf->df", rows_three, grad_upward, preferred_element_type=jnp.float32
        )
        grad_normed = reduce_grads(
            jnp.einsum("tf,df->td", grad_upward, weights[7], preferred_element_type=jnp.float32)
        )
        pull_three = jax.vjp(layer_norm, late_res, gain_vec[2], bias_vec[2])[1]
        res_part, gain_three, bias_three = pull_three(grad_normed)
        grad_res = grad_res + res_part
        grad_full = gather_grads(grad_res.astype(jnp.bfloat16))
        grad_cout = jnp.einsum(
            "tj,td->jd", merged_two, grad_full, preferred_element_type=jnp.float32
        )
        grad_merged = jnp.einsum(
            "td,jd->tj", grad_full, weights[6], preferred_element_type=jnp.float32
        ).astype(jnp.bfloat16)
        cross_gq, cross_gk, cross_gv = attend_back(
            split_heads(cross_query),
            split_heads(text_kv[0]),
            split_heads(text_kv[1]),
            log_cross,
            split_heads(grad_merged),
            cross_mask,
        )
        grad_cquery = merge_heads(cross_gq).astype(jnp.bfloat16)
        grad_text_kv = jnp.stack([merge_heads(cross_gk), merge_heads(cross_gv)]).astype(
            jnp.bfloat16
        )
        grad_cq = jnp.einsum("td,tj->dj", rows_two, grad_cquery, preferred_element_type=jnp.float32)
        grad_ckv = jnp.einsum(
            "sd,csj->dcj", text_rows, grad_text_kv, preferred_element_type=jnp.float32
        )
        text_acc = text_acc + jnp.einsum(
            "csj,dcj->sd", grad_text_kv, weights[5], preferred_element_type=jnp.float32
        )
        grad_normed = reduce_grads(
            jnp.einsum("tj,dj->td", grad_cquery, weights[4], preferred_element_type=jnp.float32)
        )
        pull_two = jax.vjp(layer_norm, mid_res, gain_vec[1], bias_vec[1])[1]
        res_part, gain_two, bias_two = pull_two(grad_normed)
        grad_res = grad_res + res_part
        grad_full = gather_grads(grad_res.astype(jnp.bfloat16))
        grad_sout = jnp.einsum(
            "tj,td->jd", merged_one, grad_full, preferred_element_type=jnp.float32
        )
        grad_merged = jnp.einsum(
            "td,jd->tj", grad_full, weights[3], preferred_element_type=jnp.float32
        ).astype(jnp.bfloat16)
        self_gq, self_gk, self_gv = attend_back(
            split_heads(queries),
            split_heads(keyvals[0]),
            split_heads(keyvals[1]),
            log_self,
            split_heads(grad_merged),
            self_mask,
        )
        key_grad_all = jnp.stack([merge_heads(self_gk), merge_heads(self_gv)])
        own_grads = key_grad_all[:, REACH * tok_count :]
        for distance in range(1, REACH + 1):
            piece = key_grad_all[
                :, (REACH - distance) * tok_count : (REACH - distance + 1) * tok_count
            ]
            own_grads = own_grads + passed_along(
                piece.astype(jnp.bfloat16), ("dp", "fsdp"), -distance
            ).astype(piece.dtype)
        grad_proj = jnp.concatenate([merge_heads(self_gq)[None], own_grads], axis=0).astype(
            jnp.bfloat16
        )
        grad_qkv = jnp.einsum(
            "td,ctj->dcj", rows_one, grad_proj, preferred_element_type=jnp.float32
        )
        grad_normed = reduce_grads(
            jnp.einsum("ctj,dcj->td", grad_proj, weights[2], preferred_element_type=jnp.float32)
        )
        pull_one = jax.vjp(layer_norm, start_res, gain_vec[0], bias_vec[0])[1]
        res_part, gain_one, bias_one = pull_one(grad_normed)
        grad_res = grad_res + res_part
        gain_rows = jnp.stack([gain_one, gain_two, gain_three])
        bias_rows = jnp.stack([bias_one, bias_two, bias_three])
        shares = (
            lax.psum_scatter(
                gain_rows.astype(jnp.bfloat16), "fsdp", scatter_dimension=1, tiled=True
            ).astype(jnp.float32),
            lax.psum_scatter(
                bias_rows.astype(jnp.bfloat16), "fsdp", scatter_dimension=1, tiled=True
            ).astype(jnp.float32),
            lax.psum_scatter(
                grad_qkv.astype(jnp.bfloat16), "fsdp", scatter_dimension=0, tiled=True
            ).astype(jnp.float32),
            lax.psum_scatter(
                grad_sout.astype(jnp.bfloat16), "fsdp", scatter_dimension=1, tiled=True
            ).astype(jnp.float32),
            lax.psum_scatter(
                grad_cq.astype(jnp.bfloat16), "fsdp", scatter_dimension=0, tiled=True
            ).astype(jnp.float32),
            lax.psum_scatter(
                grad_ckv.astype(jnp.bfloat16), "fsdp", scatter_dimension=0, tiled=True
            ).astype(jnp.float32),
            lax.psum_scatter(
                grad_cout.astype(jnp.bfloat16), "fsdp", scatter_dimension=1, tiled=True
            ).astype(jnp.float32),
            lax.psum_scatter(
                grad_up.astype(jnp.bfloat16), "fsdp", scatter_dimension=0, tiled=True
            ).astype(jnp.float32),
            lax.psum_scatter(
                grad_down.astype(jnp.bfloat16), "fsdp", scatter_dimension=1, tiled=True
            ).astype(jnp.float32),
        )
        gain_list.insert(0, shares[0])
        bias_list.insert(0, shares[1])
        summed = (
            lax.psum(shares[2].astype(jnp.bfloat16), "dp").astype(jnp.float32),
            lax.psum(shares[3].astype(jnp.bfloat16), "dp").astype(jnp.float32),
            lax.psum(shares[4].astype(jnp.bfloat16), "dp").astype(jnp.float32),
            lax.psum(shares[5].astype(jnp.bfloat16), "dp").astype(jnp.float32),
            lax.psum(shares[6].astype(jnp.bfloat16), "dp").astype(jnp.float32),
            lax.psum(shares[7].astype(jnp.bfloat16), "dp").astype(jnp.float32),
            lax.psum(shares[8].astype(jnp.bfloat16), "dp").astype(jnp.float32),
        )
        matrix_list.insert(0, summed)
    stacked = [jnp.stack([layer_set[member] for layer_set in matrix_list]) for member in range(7)]
    gain_grad, bias_grad = lax.psum((jnp.stack(gain_list), jnp.stack(bias_list)), ("dp", "mp"))
    text_full = jnp.zeros((clip_count, TEXT, model_width), jnp.float32)
    text_full = lax.dynamic_update_slice_in_dim(
        text_full, text_acc.reshape(SLOTS, TEXT, model_width), slot_first, 0
    )
    text_grad = lax.psum(text_full, ("dp", "fsdp", "mp"))
    return (
        output,
        grad_res,
        text_grad,
        gain_grad,
        bias_grad,
        stacked[0],
        stacked[1],
        stacked[2],
        stacked[3],
        stacked[4],
        stacked[5],
        stacked[6],
    )


def solution(mesh):
    in_specs = (
        P(("dp", "fsdp", "mp"), None),
        P(("dp", "fsdp")),
        P(("dp", "fsdp")),
        P(),
        P(None, None, "fsdp"),
        P(None, None, "fsdp"),
        P(None, "fsdp", None, "mp"),
        P(None, "mp", "fsdp"),
        P(None, "fsdp", "mp"),
        P(None, "fsdp", None, "mp"),
        P(None, "mp", "fsdp"),
        P(None, "fsdp", "mp"),
        P(None, "mp", "fsdp"),
        P(("dp", "fsdp", "mp"), None),
    )
    out_specs = (
        P(("dp", "fsdp", "mp"), None),
        P(("dp", "fsdp", "mp"), None),
        P(),
        P(None, None, "fsdp"),
        P(None, None, "fsdp"),
        P(None, "fsdp", None, "mp"),
        P(None, "mp", "fsdp"),
        P(None, "fsdp", "mp"),
        P(None, "fsdp", None, "mp"),
        P(None, "mp", "fsdp"),
        P(None, "fsdp", "mp"),
        P(None, "mp", "fsdp"),
    )
    return jax.shard_map(local, mesh=mesh, in_specs=in_specs, out_specs=out_specs, check_vma=False)
```

profile of v0, /device:TPU:0, one launch (start us, length us, event | category | flops | bytes accessed | tf_op | source)
XLA Modules:
  0.0 3486.2 jit_solution(16742623467894269917)
XLA Ops:
  29.5 39.5 %all-gather.45.cloned.1.call-done = bf16[640,1536]{1,0:T(8,128)(2,1)} async-done(((bf16[160,1536]{1,0:T(8,128)(2,1)}), bf16[640,1536]{1,0:T(8,128)(2,1)}) %all-gather.45.cloned.1.call-update) | async-done | bytes 1966096 | tf_op jit(solution)/shard_map/all_gather | solution.py:111
  69.0 50.4 %all-gather.69.cloned.1.call-done = bf16[1,1536,3,384]{1,3,2,0:T(8,128)(2,1)} async-done(((bf16[1,768,3,384]{1,3,2,0:T(8,128)(2,1)}), bf16[1,1536,3,384]{1,3,2,0:T(8,128)(2,1)}) %all-gather.69.cloned.1.call-update) | async-done | bytes 3538960 | tf_op jit(solution)/shard_map/all_gather | solution.py:148
  143.1 29.0 collective-permute-done.2
  183.4 66.8 %while.112 = (s32[]{:T(128)}, bf16[6,640,64]{1,2,0:T(8,128)(2,1)S(1)}, f32[6,640]{1,0:T(8,128)S(1)}, bf16[6,640,64]{2,1,0:T(8,128)(2,1)}, bf16[6,2560,64]{2,1,0:...) while((s32[]{:T(128)}, ...), condition=%wide.region_5.6_spmd.clone, body=%wide.region_2.5_spmd.clone.sunk | while | flops 437452160 | bytes 47564940 | solution.py:52
  261.0 48.4 %reduce-scatter.39.cloned.1.call-done = bf16[160,1536]{1,0:T(8,128)(2,1)} async-done(((bf16[640,1536]{1,0:T(8,128)(2,1)}), bf16[160,1536]{1,0:T(8,128)(2,1)}) %reduce-scatter.39.cloned.1.call-update) | async-done | bytes 491536 | tf_op jit(solution)/shard_map/reduce_scatter | solution.py:114
  316.6 30.1 all-gather.75.cloned.1.call-done
  349.5 22.0 all-gather.73.cloned.1.call-done
  371.5 45.7 %all-gather.47.cloned.1.call-done = bf16[640,1536]{1,0:T(8,128)(2,1)} async-done(((bf16[160,1536]{1,0:T(8,128)(2,1)}), bf16[640,1536]{1,0:T(8,128)(2,1)}) %all-gather.47.cloned.1.call-update) | async-done | bytes 1966096 | tf_op jit(solution)/shard_map/all_gather | solution.py:111
  424.7 16.2 all-gather.77.cloned.1.call-done
  449.9 36.5 %reduce-scatter.41.cloned.1.call-done = bf16[160,1536]{1,0:T(8,128)(2,1)} async-done(((bf16[640,1536]{1,0:T(8,128)(2,1)}), bf16[160,1536]{1,0:T(8,128)(2,1)}) %reduce-scatter.41.cloned.1.call-update) | async-done | bytes 491536 | tf_op jit(solution)/shard_map/reduce_scatter | solution.py:114
  494.1 56.2 %all-gather.79.cloned.1.call-done = bf16[1,1536,1536]{2,1,0:T(8,128)(2,1)} async-done(((bf16[1,768,1536]{2,1,0:T(8,128)(2,1)}), bf16[1,1536,1536]{2,1,0:T(8,128)(2,1)}) %all-gather.79.cloned.1.call-update) | async-done | bytes 4718608 | tf_op jit(solution)/shard_map/all_gather | solution.py:153
  550.3 45.7 %all-gather.49.cloned.1.call-done = bf16[640,1536]{1,0:T(8,128)(2,1)} async-done(((bf16[160,1536]{1,0:T(8,128)(2,1)}), bf16[640,1536]{1,0:T(8,128)(2,1)}) %all-gather.49.cloned.1.call-update) | async-done | bytes 1966096 | tf_op jit(solution)/shard_map/all_gather | solution.py:111
  604.1 55.4 %all-gather.81.cloned.1.call-done = bf16[1,1536,1536]{2,1,0:T(8,128)(2,1)} async-done(((bf16[1,1536,768]{2,1,0:T(8,128)(2,1)}), bf16[1,1536,1536]{2,1,0:T(8,128)(2,1)}) %all-gather.81.cloned.1.call-update) | async-done | bytes 4718608 | tf_op jit(solution)/shard_map/all_gather | solution.py:154
  680.7 28.7 reduce-scatter.43.cloned.1.call-done
  712.1 47.9 %all-gather.83.cloned.1.call-done = bf16[1,1536,3,384]{1,3,2,0:T(8,128)(2,1)} async-done(((bf16[1,768,3,384]{1,3,2,0:T(8,128)(2,1)}), bf16[1,1536,3,384]{1,3,2,0:T(8,128)(2,1)}) %all-gather.83.cloned.1.call-update) | async-done | bytes 3538960 | tf_op jit(solution)/shard_map/all_gather | solution.py:148
  760.0 45.6 %all-gather.51.cloned.1.call-done = bf16[640,1536]{1,0:T(8,128)(2,1)} async-done(((bf16[160,1536]{1,0:T(8,128)(2,1)}), bf16[640,1536]{1,0:T(8,128)(2,1)}) %all-gather.51.cloned.1.call-update) | async-done | bytes 1966096 | tf_op jit(solution)/shard_map/all_gather | solution.py:111
  833.7 25.7 collective-permute-done.5
  873.0 66.9 %while.114 = (s32[]{:T(128)}, bf16[6,640,64]{1,2,0:T(8,128)(2,1)S(1)}, f32[6,640]{1,0:T(8,128)S(1)}, bf16[6,640,64]{2,1,0:T(8,128)(2,1)}, bf16[6,2560,64]{2,1,0:...) while((s32[]{:T(128)}, ...), condition=%wide.region_22.23_spmd.clone, body=%wide.region_19.22_spmd.clone.sunk | while | flops 437452160 | bytes 47564940 | solution.py:52
  946.0 50.1 %reduce-scatter.45.cloned.1.call-done = bf16[160,1536]{1,0:T(8,128)(2,1)} async-done(((bf16[640,1536]{1,0:T(8,128)(2,1)}), bf16[160,1536]{1,0:T(8,128)(2,1)}) %reduce-scatter.45.cloned.1.call-update) | async-done | bytes 491536 | tf_op jit(solution)/shard_map/reduce_scatter | solution.py:114
  999.4 34.0 all-gather.89.cloned.1.call-done
  1036.8 20.9 all-gather.87.cloned.1.call-done
  1057.8 45.6 %all-gather.53.cloned.1.call-done = bf16[640,1536]{1,0:T(8,128)(2,1)} async-done(((bf16[160,1536]{1,0:T(8,128)(2,1)}), bf16[640,1536]{1,0:T(8,128)(2,1)}) %all-gather.53.cloned.1.call-update) | async-done | bytes 1966096 | tf_op jit(solution)/shard_map/all_gather | solution.py:111
  1107.5 15.9 while.115
  1131.1 40.9 %reduce-scatter.47.cloned.1.call-done = bf16[160,1536]{1,0:T(8,128)(2,1)} async-done(((bf16[640,1536]{1,0:T(8,128)(2,1)}), bf16[160,1536]{1,0:T(8,128)(2,1)}) %reduce-scatter.47.cloned.1.call-update) | async-done | bytes 491536 | tf_op jit(solution)/shard_map/reduce_scatter | solution.py:114
  1176.4 59.7 %all-gather.93.cloned.1.call-done = bf16[1,1536,1536]{2,1,0:T(8,128)(2,1)} async-done(((bf16[1,768,1536]{2,1,0:T(8,128)(2,1)}), bf16[1,1536,1536]{2,1,0:T(8,128)(2,1)}) %all-gather.93.cloned.1.call-update) | async-done | bytes 4718608 | tf_op jit(solution)/shard_map/all_gather | solution.py:153
  1236.1 45.6 %all-gather.55.cloned.1.call-done = bf16[640,1536]{1,0:T(8,128)(2,1)} async-done(((bf16[160,1536]{1,0:T(8,128)(2,1)}), bf16[640,1536]{1,0:T(8,128)(2,1)}) %all-gather.55.cloned.1.call-update) | async-done | bytes 1966096 | tf_op jit(solution)/shard_map/all_gather | solution.py:111
  1289.8 35.9 %all-gather.57.cloned.1.call-done = bf16[640,1536]{1,0:T(8,128)(2,1)} async-done(((bf16[160,1536]{1,0:T(8,128)(2,1)}), bf16[640,1536]{1,0:T(8,128)(2,1)}) %all-gather.57.cloned.1.call-update) | async-done | bytes 1966096 | tf_op jit(solution)/shard_map/all_gather | solution.py:119
  1325.7 63.5 %all-gather.95.cloned.1.call-done = bf16[1,1536,1536]{2,1,0:T(8,128)(2,1)} async-done(((bf16[1,1536,768]{2,1,0:T(8,128)(2,1)}), bf16[1,1536,1536]{2,1,0:T(8,128)(2,1)}) %all-gather.95.cloned.1.call-update) | async-done | bytes 4718608 | tf_op jit(solution)/shard_map/all_gather | solution.py:154
  1414.9 33.2 reduce-scatter.51.cloned.1.call-done
  1450.2 41.6 %reduce-scatter.49.cloned.1.call-done = bf16[160,1536]{1,0:T(8,128)(2,1)} async-done(((bf16[640,1536]{1,0:T(8,128)(2,1)}), bf16[160,1536]{1,0:T(8,128)(2,1)}) %reduce-scatter.49.cloned.1.call-update) | async-done | bytes 491536 | tf_op jit(solution)/shard_map/reduce_scatter | solution.py:114
  1496.1 42.9 %all-gather.59.cloned.1.call-done = bf16[640,1536]{1,0:T(8,128)(2,1)} async-done(((bf16[160,1536]{1,0:T(8,128)(2,1)}), bf16[640,1536]{1,0:T(8,128)(2,1)}) %all-gather.59.cloned.1.call-update) | async-done | bytes 1966096 | tf_op jit(solution)/shard_map/all_gather | solution.py:119
  1543.3 31.5 while.116
  1578.9 40.4 %reduce-scatter.53.cloned.1.call-done = bf16[160,1536]{1,0:T(8,128)(2,1)} async-done(((bf16[640,1536]{1,0:T(8,128)(2,1)}), bf16[160,1536]{1,0:T(8,128)(2,1)}) %reduce-scatter.53.cloned.1.call-update) | async-done | bytes 491536 | tf_op jit(solution)/shard_map/reduce_scatter | solution.py:122
  1625.7 42.7 %all-gather.61.cloned.1.call-done = bf16[640,1536]{1,0:T(8,128)(2,1)} async-done(((bf16[160,1536]{1,0:T(8,128)(2,1)}), bf16[640,1536]{1,0:T(8,128)(2,1)}) %all-gather.61.cloned.1.call-update) | async-done | bytes 1966096 | tf_op jit(solution)/shard_map/all_gather | solution.py:119
  1677.6 87.9 %while.117 = (s32[]{:T(128)}, bf16[6,640,64]{1,2,0:T(8,128)(2,1)S(1)}, f32[6,2560,64]{1,2,0:T(8,128)}, f32[6,2560,64]{1,2,0:T(8,128)}, bf16[6,640,64]{2,1,0:T(8,...) while((s32[]{:T(128)}, ...), condition=%wide.region_45.46_spmd.clone, body=%wide.region_43.45_spmd.clone.sunk | while | flops 1068440960 | bytes 53281408 | solution.py:83
  1786.1 33.1 collective-permute-done.6
  1819.2 9.5 collective-permute-done.8
  1836.2 41.1 %reduce-scatter.55.cloned.1.call-done = bf16[160,1536]{1,0:T(8,128)(2,1)} async-done(((bf16[640,1536]{1,0:T(8,128)(2,1)}), bf16[160,1536]{1,0:T(8,128)(2,1)}) %reduce-scatter.55.cloned.1.call-update) | async-done | bytes 491536 | tf_op jit(solution)/shard_map/reduce_scatter | solution.py:122
  1883.0 42.7 %all-gather.63.cloned.1.call-done = bf16[640,1536]{1,0:T(8,128)(2,1)} async-done(((bf16[160,1536]{1,0:T(8,128)(2,1)}), bf16[640,1536]{1,0:T(8,128)(2,1)}) %all-gather.63.cloned.1.call-update) | async-done | bytes 1966096 | tf_op jit(solution)/shard_map/all_gather | solution.py:119
  1943.2 40.4 %reduce-scatter.57.cloned.1.call-done = bf16[160,1536]{1,0:T(8,128)(2,1)} async-done(((bf16[640,1536]{1,0:T(8,128)(2,1)}), bf16[160,1536]{1,0:T(8,128)(2,1)}) %reduce-scatter.57.cloned.1.call-update) | async-done | bytes 491536 | tf_op jit(solution)/shard_map/reduce_scatter | solution.py:122
  1990.1 42.9 %all-gather.65.cloned.1.call-done = bf16[640,1536]{1,0:T(8,128)(2,1)} async-done(((bf16[160,1536]{1,0:T(8,128)(2,1)}), bf16[640,1536]{1,0:T(8,128)(2,1)}) %all-gather.65.cloned.1.call-update) | async-done | bytes 1966096 | tf_op jit(solution)/shard_map/all_gather | solution.py:119
  2036.5 32.4 while.118
  2073.5 40.4 %reduce-scatter.59.cloned.1.call-done = bf16[160,1536]{1,0:T(8,128)(2,1)} async-done(((bf16[640,1536]{1,0:T(8,128)(2,1)}), bf16[160,1536]{1,0:T(8,128)(2,1)}) %reduce-scatter.59.cloned.1.call-update) | async-done | bytes 491536 | tf_op jit(solution)/shard_map/reduce_scatter | solution.py:122
  2120.4 42.5 %all-gather.67.cloned.1.call-done = bf16[640,1536]{1,0:T(8,128)(2,1)} async-done(((bf16[160,1536]{1,0:T(8,128)(2,1)}), bf16[640,1536]{1,0:T(8,128)(2,1)}) %all-gather.67.cloned.1.call-update) | async-done | bytes 1966096 | tf_op jit(solution)/shard_map/all_gather | solution.py:119
  2171.7 87.8 %while.119 = (s32[]{:T(128)}, bf16[6,640,64]{1,2,0:T(8,128)(2,1)S(1)}, f32[6,2560,64]{1,2,0:T(8,128)}, f32[6,2560,64]{1,2,0:T(8,128)}, bf16[6,640,64]{2,1,0:T(8,...) while((s32[]{:T(128)}, ...), condition=%wide.region_60.61_spmd.clone, body=%wide.region_58.60_spmd.clone.sunk | while | flops 1068440960 | bytes 53281408 | solution.py:83
  2280.5 32.7 collective-permute-done.11
  2418.7 62.9 %reduce-scatter.85.cloned.1.call-done = bf16[768,1536]{1,0:T(8,128)(2,1)} async-done(((bf16[1536,1536]{1,0:T(8,128)(2,1)}), bf16[768,1536]{1,0:T(8,128)(2,1)}) %reduce-scatter.85.cloned.1.call-update) | async-done | bytes 2359312 | tf_op jit(solution)/shard_map/reduce_scatter | solution.py:368
  2481.6 63.0 %reduce-scatter.89.cloned.1.call-done = bf16[1536,768]{1,0:T(8,128)(2,1)} async-done(((bf16[1536,1536]{1,0:T(8,128)(2,1)}), bf16[1536,768]{1,0:T(8,128)(2,1)}) %reduce-scatter.89.cloned.1.call-update) | async-done | bytes 2359312 | tf_op jit(solution)/shard_map/reduce_scatter | solution.py:371
  2544.6 37.4 %reduce-scatter.77.cloned.1.call-done = bf16[768,2,384]{2,0,1:T(8,128)(2,1)} async-done(((bf16[1536,2,384]{2,0,1:T(8,128)(2,1)}), bf16[768,2,384]{2,0,1:T(8,128)(2,1)}) %reduce-scatter.77.cloned.1.call-update) | async-done | bytes 1179664 | tf_op jit(solution)/shard_map/reduce_scatter | solution.py:362
  2582.1 24.7 reduce-scatter.69.cloned.1.call-done
  2606.8 49.8 %reduce-scatter.65.cloned.1.call-done = bf16[768,3,384]{2,0,1:T(8,128)(2,1)} async-done(((bf16[1536,3,384]{2,0,1:T(8,128)(2,1)}), bf16[768,3,384]{2,0,1:T(8,128)(2,1)}) %reduce-scatter.65.cloned.1.call-update) | async-done | bytes 1769488 | tf_op jit(solution)/shard_map/reduce_scatter | solution.py:353
  2656.6 24.0 reduce-scatter.79.cloned.1.call-done
  2680.6 23.9 reduce-scatter.71.cloned.1.call-done
  2704.4 62.8 %reduce-scatter.87.cloned.1.call-done = bf16[1536,768]{1,0:T(8,128)(2,1)} async-done(((bf16[1536,1536]{1,0:T(8,128)(2,1)}), bf16[1536,768]{1,0:T(8,128)(2,1)}) %reduce-scatter.87.cloned.1.call-update) | async-done | bytes 2359312 | tf_op jit(solution)/shard_map/reduce_scatter | solution.py:371
  2767.3 62.8 %reduce-scatter.83.cloned.1.call-done = bf16[768,1536]{1,0:T(8,128)(2,1)} async-done(((bf16[1536,1536]{1,0:T(8,128)(2,1)}), bf16[768,1536]{1,0:T(8,128)(2,1)}) %reduce-scatter.83.cloned.1.call-update) | async-done | bytes 2359312 | tf_op jit(solution)/shard_map/reduce_scatter | solution.py:368
  2830.0 37.7 %reduce-scatter.75.cloned.1.call-done = bf16[768,2,384]{2,0,1:T(8,128)(2,1)} async-done(((bf16[1536,2,384]{2,0,1:T(8,128)(2,1)}), bf16[768,2,384]{2,0,1:T(8,128)(2,1)}) %reduce-scatter.75.cloned.1.call-update) | async-done | bytes 1179664 | tf_op jit(solution)/shard_map/reduce_scatter | solution.py:362
  2867.7 23.9 reduce-scatter.67.cloned.1.call-done
  2891.6 50.0 %reduce-scatter.63.cloned.1.call-done = bf16[768,3,384]{2,0,1:T(8,128)(2,1)} async-done(((bf16[1536,3,384]{2,0,1:T(8,128)(2,1)}), bf16[768,3,384]{2,0,1:T(8,128)(2,1)}) %reduce-scatter.63.cloned.1.call-update) | async-done | bytes 1769488 | tf_op jit(solution)/shard_map/reduce_scatter | solution.py:353
  2941.9 15.0 reduce-scatter.97.cloned.1.call-done
  2957.9 15.1 reduce-scatter.93.cloned.1.call-done
  2989.4 15.1 reduce-scatter.91.cloned.1.call-done
  3005.5 63.0 %all-reduce = (f32[2,3,768]{2,1,0:T(4,128)S(1)}, f32[2,3,768]{2,1,0:T(4,128)S(1)}) all-reduce(f32[2,3,768]{2,1,0:T(4,128)S(1)} %maximum_convert_fusion.7, f32[2,3,768]{2,1,0:T(4,128)S(1)} %maximum_convert_fusion.8), channel_id=1, replica_groups=mesh['dp'=4,'fsdp'=2,'mp'=4] {'dp','mp'}, use_global_device_ids=true, to_apply=%region_73.74 | all-reduce | flops 9216 | bytes 73728 | tf_op jit(solution)/shard_map/psum | solution.py:388
  3069.8 268.1 %all-reduce.7.cloned.1.call-done = (bf16[1,768,3,384]{3,1,2,0:T(8,128)(2,1)}, bf16[1,768,3,384]{3,1,2,0:T(8,128)(2,1)}, bf16[1,384,768]{2,1,0:T(8,128)(2,1)}, bf...) async-done(((bf16[1,768,3,384]{3,1,2,0:T(8,128)(2,1)}, ...) | async-done | bytes 18874384 | tf_op jit(solution)/shard_map/psum | solution.py:378
  3364.3 112.5 %all-reduce.5.cloned.1.call-done = f32[4,64,1536]{2,1,0:T(8,128)} async-done(((f32[4,64,1536]{2,1,0:T(8,128)}), f32[4,64,1536]{2,1,0:T(8,128)}) %all-reduce.5.cloned.1.call-update) | async-done | bytes 1572880 | tf_op jit(solution)/shard_map/psum | solution.py:393
  (992 shorter events, 913.6 us)
Async XLA Ops:
  7.2 61.8 %all-gather.45.cloned.1.call-start = ((), (), s32[]{:S(2)}) async-start(), calls=%async_computation.30 | async-start | bytes 2457600 | tf_op jit(solution)/shard_map/all_gather | solution.py:111
  23.5 95.8 %all-gather.69.cloned.1.call-start = ((), (), s32[]{:S(2)}) async-start(), calls=%async_computation.69 | async-start | bytes 5308416 | tf_op jit(solution)/shard_map/all_gather | solution.py:148
  29.4 220.9 %all-gather.71.cloned.1.call-start = ((), (), s32[]{:S(2)}) async-start(), calls=%async_computation.70 | async-start | bytes 1769472 | tf_op jit(solution)/shard_map/all_gather | solution.py:149
  132.3 39.8 %collective-permute-start.2 = (bf16[2,640,384]{1,2,0:T(8,128)(2,1)S(1)}, bf16[2,640,384]{1,2,0:T(8,128)(2,1)}, u32[]{:S(2)}, u32[]{:S(2)}) collective-permute-start(bf16[2,640,384]{1,2,0:T(8,128)(2,1)S(1)} %slice.261), channel_id=1, source_target_pairs={{0,4},{4,8},{8,12},{12,16},{16,20},{20,24},{24,28},{1,5},{5,9},{9,... | collective-permute-start | bytes 2949128 | tf_op jit(solution)/shard_map/ppermute | solution.py:20
  137.0 172.3 %reduce-scatter.39.cloned.1.call-start = ((), (), s32[]{:S(2)}) async-start(), calls=%async_computation.31 | async-start | bytes 2457600 | tf_op jit(solution)/shard_map/reduce_scatter | solution.py:114
  255.1 91.6 %all-gather.75.cloned.1.call-start = ((), (), s32[]{:S(2)}) async-start(), calls=%async_computation.72 | async-start | bytes 3538944 | tf_op jit(solution)/shard_map/all_gather | solution.py:151
  259.3 112.2 %all-gather.73.cloned.1.call-start = ((), (), s32[]{:S(2)}) async-start(), calls=%async_computation.71 | async-start | bytes 1769472 | tf_op jit(solution)/shard_map/all_gather | solution.py:150
  260.9 156.3 %all-gather.47.cloned.1.call-start = ((), (), s32[]{:S(2)}) async-start(), calls=%async_computation.32 | async-start | bytes 2457600 | tf_op jit(solution)/shard_map/all_gather | solution.py:111
  314.1 126.9 %all-gather.77.cloned.1.call-start = ((), (), s32[]{:S(2)}) async-start(), calls=%async_computation.73 | async-start | bytes 1769472 | tf_op jit(solution)/shard_map/all_gather | solution.py:152
  315.3 171.1 %reduce-scatter.41.cloned.1.call-start = ((), (), s32[]{:S(2)}) async-start(), calls=%async_computation.33 | async-start | bytes 2457600 | tf_op jit(solution)/shard_map/reduce_scatter | solution.py:114
  444.8 105.4 %all-gather.79.cloned.1.call-start = ((), (), s32[]{:S(2)}) async-start(), calls=%async_computation.74 | async-start | bytes 7077888 | tf_op jit(solution)/shard_map/all_gather | solution.py:153
  449.8 146.2 %all-gather.49.cloned.1.call-start = ((), (), s32[]{:S(2)}) async-start(), calls=%async_computation.34 | async-start | bytes 2457600 | tf_op jit(solution)/shard_map/all_gather | solution.py:111
  489.1 170.4 %all-gather.81.cloned.1.call-start = ((), (), s32[]{:S(2)}) async-start(), calls=%async_computation.75 | async-start | bytes 7077888 | tf_op jit(solution)/shard_map/all_gather | solution.py:154
  494.0 215.4 %reduce-scatter.43.cloned.1.call-start = ((), (), s32[]{:S(2)}) async-start(), calls=%async_computation.35 | async-start | bytes 2457600 | tf_op jit(solution)/shard_map/reduce_scatter | solution.py:114
  667.8 92.2 %all-gather.83.cloned.1.call-start = ((), (), s32[]{:S(2)}) async-start(), calls=%async_computation.76 | async-start | bytes 5308416 | tf_op jit(solution)/shard_map/all_gather | solution.py:148
  671.7 133.9 %all-gather.51.cloned.1.call-start = ((), (), s32[]{:S(2)}) async-start(), calls=%async_computation.36 | async-start | bytes 2457600 | tf_op jit(solution)/shard_map/all_gather | solution.py:111
  712.0 227.9 %all-gather.85.cloned.1.call-start = ((), (), s32[]{:S(2)}) async-start(), calls=%async_computation.77 | async-start | bytes 1769472 | tf_op jit(solution)/shard_map/all_gather | solution.py:149
  819.5 39.9 %collective-permute-start.5 = (bf16[2,640,384]{1,2,0:T(8,128)(2,1)S(1)}, bf16[2,640,384]{1,2,0:T(8,128)(2,1)}, u32[]{:S(2)}, u32[]{:S(2)}) collective-permute-start(bf16[2,640,384]{1,2,0:T(8,128)(2,1)S(1)} %slice.273), channel_id=1, source_target_pairs={{0,4},{4,8},{8,12},{12,16},{16,20},{20,24},{24,28},{1,5},{5,9},{9,... | collective-permute-start | bytes 2949128 | tf_op jit(solution)/shard_map/ppermute | solution.py:20
  822.2 173.9 %reduce-scatter.45.cloned.1.call-start = ((), (), s32[]{:S(2)}) async-start(), calls=%async_computation.37 | async-start | bytes 2457600 | tf_op jit(solution)/shard_map/reduce_scatter | solution.py:114
  943.9 89.5 %all-gather.89.cloned.1.call-start = ((), (), s32[]{:S(2)}) async-start(), calls=%async_computation.79 | async-start | bytes 3538944 | tf_op jit(solution)/shard_map/all_gather | solution.py:151
  945.2 112.6 %all-gather.87.cloned.1.call-start = ((), (), s32[]{:S(2)}) async-start(), calls=%async_computation.78 | async-start | bytes 1769472 | tf_op jit(solution)/shard_map/all_gather | solution.py:150
  946.0 157.4 %all-gather.53.cloned.1.call-start = ((), (), s32[]{:S(2)}) async-start(), calls=%async_computation.38 | async-start | bytes 2457600 | tf_op jit(solution)/shard_map/all_gather | solution.py:111
  998.7 127.9 %all-gather.91.cloned.1.call-start = ((), (), s32[]{:S(2)}) async-start(), calls=%async_computation.80 | async-start | bytes 1769472 | tf_op jit(solution)/shard_map/all_gather | solution.py:152
  999.4 172.6 %reduce-scatter.47.cloned.1.call-start = ((), (), s32[]{:S(2)}) async-start(), calls=%async_computation.39 | async-start | bytes 2457600 | tf_op jit(solution)/shard_map/reduce_scatter | solution.py:114
  1130.3 105.7 %all-gather.93.cloned.1.call-start = ((), (), s32[]{:S(2)}) async-start(), calls=%async_computation.81 | async-start | bytes 7077888 | tf_op jit(solution)/shard_map/all_gather | solution.py:153
  1131.1 150.6 %all-gather.55.cloned.1.call-start = ((), (), s32[]{:S(2)}) async-start(), calls=%async_computation.40 | async-start | bytes 2457600 | tf_op jit(solution)/shard_map/all_gather | solution.py:111
  1174.6 151.1 %all-gather.57.cloned.1.call-start = ((), (), s32[]{:S(2)}) async-start(), calls=%async_computation.42 | async-start | bytes 2457600 | tf_op jit(solution)/shard_map/all_gather | solution.py:119
  1175.4 213.8 %all-gather.95.cloned.1.call-start = ((), (), s32[]{:S(2)}) async-start(), calls=%async_computation.82 | async-start | bytes 7077888 | tf_op jit(solution)/shard_map/all_gather | solution.py:154
  1176.0 272.2 %reduce-scatter.51.cloned.1.call-start = ((), (), s32[]{:S(2)}) async-start(), calls=%async_computation.43 | async-start | bytes 2457600 | tf_op jit(solution)/shard_map/reduce_scatter | solution.py:122
  1406.6 85.2 %reduce-scatter.49.cloned.1.call-start = ((), (), s32[]{:S(2)}) async-start(), calls=%async_computation.41 | async-start | bytes 2457600 | tf_op jit(solution)/shard_map/reduce_scatter | solution.py:114
  1414.9 124.1 %all-gather.59.cloned.1.call-start = ((), (), s32[]{:S(2)}) async-start(), calls=%async_computation.44 | async-start | bytes 2457600 | tf_op jit(solution)/shard_map/all_gather | solution.py:119
  1496.0 123.3 %reduce-scatter.53.cloned.1.call-start = ((), (), s32[]{:S(2)}) async-start(), calls=%async_computation.45 | async-start | bytes 2457600 | tf_op jit(solution)/shard_map/reduce_scatter | solution.py:122
  1578.9 89.5 %all-gather.61.cloned.1.call-start = ((), (), s32[]{:S(2)}) async-start(), calls=%async_computation.46 | async-start | bytes 2457600 | tf_op jit(solution)/shard_map/all_gather | solution.py:119
  1625.5 251.9 %reduce-scatter.55.cloned.1.call-start = ((), (), s32[]{:S(2)}) async-start(), calls=%async_computation.47 | async-start | bytes 2457600 | tf_op jit(solution)/shard_map/reduce_scatter | solution.py:122
  1781.9 37.3 %collective-permute-start.6 = (bf16[2,640,384]{2,1,0:T(8,128)(2,1)}, bf16[2,640,384]{2,1,0:T(8,128)(2,1)S(1)}, u32[]{:S(2)}, u32[]{:S(2)}) collective-permute-start(bf16[2,640,384]{2,1,0:T(8,128)(2,1)} %get-tuple-element.947), channel_id=1, source_target_pairs={{4,0},{8,4},{12,8},{16,12},{20,16},{24,20},{28,24},{5,1},{9,5},{13... | collective-permute-start | bytes 2949128 | tf_op jit(solution)/shard_map/ppermute | solution.py:20
  1784.5 44.2 %collective-permute-start.8 = (bf16[2,640,384]{2,1,0:T(8,128)(2,1)S(1)}, bf16[2,640,384]{2,1,0:T(8,128)(2,1)}, u32[]{:S(2)}, u32[]{:S(2)}) collective-permute-start(bf16[2,640,384]{2,1,0:T(8,128)(2,1)S(1)} %get-tuple-element.948), channel_id=1, source_target_pairs={{12,0},{16,4},{20,8},{24,12},{28,16},{13,1},{17,5},{21,9},{25,13},... | collective-permute-start | bytes 2949128 | tf_op jit(solution)/shard_map/ppermute | solution.py:20
  1836.1 89.6 %all-gather.63.cloned.1.call-start = ((), (), s32[]{:S(2)}) async-start(), calls=%async_computation.48 | async-start | bytes 2457600 | tf_op jit(solution)/shard_map/all_gather | solution.py:119
  1882.7 100.9 %reduce-scatter.57.cloned.1.call-start = ((), (), s32[]{:S(2)}) async-start(), calls=%async_computation.49 | async-start | bytes 2457600 | tf_op jit(solution)/shard_map/reduce_scatter | solution.py:122
  1943.2 89.8 %all-gather.65.cloned.1.call-start = ((), (), s32[]{:S(2)}) async-start(), calls=%async_computation.50 | async-start | bytes 2457600 | tf_op jit(solution)/shard_map/all_gather | solution.py:119
  1990.0 123.8 %reduce-scatter.59.cloned.1.call-start = ((), (), s32[]{:S(2)}) async-start(), calls=%async_computation.51 | async-start | bytes 2457600 | tf_op jit(solution)/shard_map/reduce_scatter | solution.py:122
  2073.4 89.4 %all-gather.67.cloned.1.call-start = ((), (), s32[]{:S(2)}) async-start(), calls=%async_computation.52 | async-start | bytes 2457600 | tf_op jit(solution)/shard_map/all_gather | solution.py:119
  2119.9 286.1 %reduce-scatter.61.cloned.1.call-start = ((), (), s32[]{:S(2)}) async-start(), calls=%async_computation.53 | async-start | bytes 2457600 | tf_op jit(solution)/shard_map/reduce_scatter | solution.py:122
  2277.1 36.0 %collective-permute-start.11 = (bf16[2,640,384]{2,1,0:T(8,128)(2,1)}, bf16[2,640,384]{2,1,0:T(8,128)(2,1)}, u32[]{:S(2)}, u32[]{:S(2)}) collective-permute-start(bf16[2,640,384]{2,1,0:T(8,128)(2,1)} %get-tuple-element.945), channel_id=1, source_target_pairs={{12,0},{16,4},{20,8},{24,12},{28,16},{13,1},{17,5},{21,9},{25,13},... | collective-permute-start | bytes 2949128 | tf_op jit(solution)/shard_map/ppermute | solution.py:20
  2278.4 37.2 %collective-permute-start.9 = (bf16[2,640,384]{2,1,0:T(8,128)(2,1)S(1)}, bf16[2,640,384]{2,1,0:T(8,128)(2,1)}, u32[]{:S(2)}, u32[]{:S(2)}) collective-permute-start(bf16[2,640,384]{2,1,0:T(8,128)(2,1)S(1)} %get-tuple-element.944), channel_id=1, source_target_pairs={{4,0},{8,4},{12,8},{16,12},{20,16},{24,20},{28,24},{5,1},{9,5},{13... | collective-permute-start | bytes 2949128 | tf_op jit(solution)/shard_map/ppermute | solution.py:20
  2322.1 90.4 %reduce-scatter.81.cloned.1.call-start = ((), (), s32[]{:S(2)}) async-start(), calls=%async_computation.64 | async-start | bytes 1769472 | tf_op jit(solution)/shard_map/reduce_scatter | solution.py:365
  2325.8 92.9 %reduce-scatter.73.cloned.1.call-start = ((), (), s32[]{:S(2)}) async-start(), calls=%async_computation.60 | async-start | bytes 1769472 | tf_op jit(solution)/shard_map/reduce_scatter | solution.py:359
  2330.0 151.7 %reduce-scatter.85.cloned.1.call-start = ((), (), s32[]{:S(2)}) async-start(), calls=%async_computation.66 | async-start | bytes 7077888 | tf_op jit(solution)/shard_map/reduce_scatter | solution.py:368
  2338.2 206.4 %reduce-scatter.89.cloned.1.call-start = ((), (), s32[]{:S(2)}) async-start(), calls=%async_computation.68 | async-start | bytes 7077888 | tf_op jit(solution)/shard_map/reduce_scatter | solution.py:371
  2347.4 234.7 %reduce-scatter.77.cloned.1.call-start = ((), (), s32[]{:S(2)}) async-start(), calls=%async_computation.62 | async-start | bytes 3538944 | tf_op jit(solution)/shard_map/reduce_scatter | solution.py:362
  2350.8 256.0 %reduce-scatter.69.cloned.1.call-start = ((), (), s32[]{:S(2)}) async-start(), calls=%async_computation.58 | async-start | bytes 1769472 | tf_op jit(solution)/shard_map/reduce_scatter | solution.py:356
  2354.7 301.8 %reduce-scatter.65.cloned.1.call-start = ((), (), s32[]{:S(2)}) async-start(), calls=%async_computation.56 | async-start | bytes 5308416 | tf_op jit(solution)/shard_map/reduce_scatter | solution.py:353
  2361.6 319.0 %reduce-scatter.79.cloned.1.call-start = ((), (), s32[]{:S(2)}) async-start(), calls=%async_computation.63 | async-start | bytes 1769472 | tf_op jit(solution)/shard_map/reduce_scatter | solution.py:365
  2366.3 338.2 %reduce-scatter.71.cloned.1.call-start = ((), (), s32[]{:S(2)}) async-start(), calls=%async_computation.59 | async-start | bytes 1769472 | tf_op jit(solution)/shard_map/reduce_scatter | solution.py:359
  2370.3 397.0 %reduce-scatter.87.cloned.1.call-start = ((), (), s32[]{:S(2)}) async-start(), calls=%async_computation.67 | async-start | bytes 7077888 | tf_op jit(solution)/shard_map/reduce_scatter | solution.py:371
  2379.5 450.5 %reduce-scatter.83.cloned.1.call-start = ((), (), s32[]{:S(2)}) async-start(), calls=%async_computation.65 | async-start | bytes 7077888 | tf_op jit(solution)/shard_map/reduce_scatter | solution.py:368
  2388.2 479.5 %reduce-scatter.75.cloned.1.call-start = ((), (), s32[]{:S(2)}) async-start(), calls=%async_computation.61 | async-start | bytes 3538944 | tf_op jit(solution)/shard_map/reduce_scatter | solution.py:362
  2391.6 500.0 %reduce-scatter.67.cloned.1.call-start = ((), (), s32[]{:S(2)}) async-start(), calls=%async_computation.57 | async-start | bytes 1769472 | tf_op jit(solution)/shard_map/reduce_scatter | solution.py:356
  2395.3 546.3 %reduce-scatter.63.cloned.1.call-start = ((), (), s32[]{:S(2)}) async-start(), calls=%async_computation.55 | async-start | bytes 5308416 | tf_op jit(solution)/shard_map/reduce_scatter | solution.py:353
  2402.1 554.8 %reduce-scatter.97.cloned.1.call-start = ((), (), s32[]{:S(2)}) async-start(), calls=%async_computation.86 | async-start | bytes 589824
  2404.7 568.3 %reduce-scatter.93.cloned.1.call-start = ((), (), s32[]{:S(2)}) async-start(), calls=%async_computation.84 | async-start | bytes 589824
  2405.7 582.6 %reduce-scatter.95.cloned.1.call-start = ((), (), s32[]{:S(2)}) async-start(), calls=%async_computation.85 | async-start | bytes 589824
  2411.3 593.1 %reduce-scatter.91.cloned.1.call-start = ((), (), s32[]{:S(2)}) async-start(), calls=%async_computation.83 | async-start | bytes 589824
  2412.4 925.5 %all-reduce.7.cloned.1.call-start = ((), (), s32[]{:S(2)}) async-start(), calls=%async_computation.87 | async-start | bytes 37748736 | tf_op jit(solution)/shard_map/psum | solution.py:378
  2941.6 535.2 %all-reduce.5.cloned.1.call-start = ((), (), s32[]{:S(2)}) async-start(), calls=%async_computation.54 | async-start | bytes 3145728 | tf_op jit(solution)/shard_map/psum | solution.py:393
  (153 other events, 4784.2 us)
Sparse Core Ops, SparseCore 0:
  23.6 45.3 all-gather.44
  71.1 48.1 all-gather.68
  137.2 31.3 all-gather.70
  255.2 54.0 reduce-scatter.38
  311.4 35.2 all-gather.74
  348.7 22.7 all-gather.72
  373.6 43.5 all-gather.46
  419.3 21.6 all-gather.76
  444.9 41.4 reduce-scatter.40
  488.3 61.8 all-gather.78
  552.4 43.5 all-gather.48
  598.0 61.4 all-gather.80
  667.9 41.4 reduce-scatter.42
  711.4 48.5 all-gather.82
  762.0 43.5 all-gather.50
  822.3 30.2 all-gather.84
  944.0 52.0 reduce-scatter.44
  998.1 35.3 all-gather.88
  1034.9 22.7 all-gather.86
  1059.8 43.5 all-gather.52
  1104.9 21.6 all-gather.90
  1130.4 41.5 reduce-scatter.46
  1174.2 61.8 all-gather.92
  1238.1 43.5 all-gather.54
  1283.3 42.3 all-gather.56
  1327.7 61.4 all-gather.94
  1406.7 41.4 reduce-scatter.50
  1451.1 40.6 reduce-scatter.48
  1496.1 42.7 all-gather.58
  1579.0 40.2 reduce-scatter.52
  1625.6 42.7 all-gather.60
  1836.3 41.0 reduce-scatter.54
  1882.9 42.8 all-gather.62
  1943.3 40.2 reduce-scatter.56
  1990.2 42.7 all-gather.64
  2073.5 40.2 reduce-scatter.58
  2120.1 42.7 all-gather.66
  2322.2 49.3 reduce-scatter.60
  2373.6 20.9 reduce-scatter.80
  2397.0 21.7 reduce-scatter.72
  2421.6 59.9 reduce-scatter.84
  2484.6 59.9 reduce-scatter.88
  2547.3 34.7 reduce-scatter.76
  2585.0 21.7 reduce-scatter.68
  2608.9 47.6 reduce-scatter.64
  2658.7 21.7 reduce-scatter.78
  2682.6 21.7 reduce-scatter.70
  2707.3 59.9 reduce-scatter.86
  2770.0 59.9 reduce-scatter.82
  2832.9 34.7 reduce-scatter.74
  2869.8 21.7 reduce-scatter.66
  2893.9 47.6 reduce-scatter.62
  2943.7 13.1 reduce-scatter.96
  2959.8 13.1 reduce-scatter.92
  2975.2 13.0 reduce-scatter.94
  2991.2 13.1 reduce-scatter.90
  3008.5 329.2 all-reduce.6
  3344.4 132.3 all-reduce.4
where the time goes:
time: 3500 us; the launch traced here: 3490 us
  waiting for transfers between devices  2520 us (72%)
  matrix products  518 us (15%)
  local copies, waits for them, and re-layouts  193 us (6%)
  other arithmetic  112 us (3%)
  blocking collectives  81.4 us (2%)
  starting transfers between devices  43 us (1%)
    psum x1, waiting for transfers between devices, local(): lax.psum(shares[2].astype(jnp.bfloat16), 'dp').astype(jnp.float32)  268 us
    all_gather x6, waiting for transfers between devices, spread_rows(): return lax.all_gather(values, 'mp', axis=0, tiled=True)  268 us
    all_gather x6, waiting for transfers between devices, gather_grads(): return lax.all_gather(values, 'mp', axis=0, tiled=True)  250 us
    reduce_scatter x6, waiting for transfers between devices, reduce_rows(): lax.psum_scatter(values.astype(jnp.bfloat16), 'mp', scatter_dimension=0,...  246 us
    reduce_scatter x6, waiting for transfers between devices, reduce_grads(): lax.psum_scatter(values.astype(jnp.bfloat16), 'mp', scatter_dimension=0,...  196 us
    ppermute x12, waiting for transfers between devices, passed_along(): lax.ppermute(value, axis, [(source, source + steps) for source in range(l...  137 us
    reduce_scatter x2, waiting for transfers between devices, local(): lax.psum_scatter(grad_down.astype(jnp.bfloat16), 'fsdp', scatter_dimensio...  126 us
    reduce_scatter x2, waiting for transfers between devices, local(): lax.psum_scatter(grad_up.astype(jnp.bfloat16), 'fsdp', scatter_dimension=...  126 us
  transfers between devices with their start and end apart: 70, of which 63 were waited for; matrix products, arithmetic and copies ran while one was open for 10% of the time, Pallas kernels for 0%

commit v1 on v0

v1 whole, which is shorter than its diff:
```python
import functools

import jax
import jax.numpy as jnp
from jax import lax
from jax.experimental import pallas as pl
from jax.experimental.pallas import tpu as pltpu
from jax.sharding import PartitionSpec as P

HEAD_DIM = 64
TEXT = 64
SLOTS = 2
REACH = 3
CLIP_HI = 1536
LANES = 128

norm_eps = 1e-05
score_scale = 0.125
masked_fill = -1e30
gelu_root = 0.7978845608028654
gelu_cubic = 0.044715
bf16 = jnp.bfloat16
f32 = jnp.float32
NT = (((1,), (1,)), ((), ()))
NN = (((1,), (0,)), ((), ()))
TN = (((0,), (0,)), ((), ()))


def mm(a, b, dims=NN):
    return lax.dot_general(a, b, dims, preferred_element_type=f32)


def passed_along(value, axis, steps):
    count = lax.axis_size(axis)
    leading, last = (max(0, -steps), min(count, count - steps))
    return lax.ppermute(value, axis, [(source, source + steps) for source in range(leading, last)])


def swapped(value, axis, mask):
    count = lax.axis_size(axis)
    return lax.ppermute(value, axis, [(source, source ^ mask) for source in range(count)])


def ordered(bit, own, other, axis):
    lower = jnp.where(bit == 0, own, other)
    upper = jnp.where(bit == 0, other, own)
    return jnp.concatenate([lower, upper], axis=axis)


def part_of(value, index, size, axis):
    return lax.dynamic_slice_in_dim(value, index * size, size, axis)


def stack_heads(block):
    lane = lax.broadcasted_iota(jnp.int32, block.shape, 1)
    zero = jnp.zeros_like(block)
    return jnp.concatenate(
        [jnp.where(lane < HEAD_DIM, block, zero), jnp.where(lane < HEAD_DIM, zero, block)], axis=0
    )


def unstack_heads(block):
    rows = block.shape[0] // 2
    lane = lax.broadcasted_iota(jnp.int32, (rows, block.shape[1]), 1)
    return jnp.where(lane < HEAD_DIM, block[:rows], block[rows:])


def self_forward_kernel(sizes, cs_ref, q_ref, k0, v0, k1, v1, k2, v2, k3, v3, o_ref, lse_ref):
    tok, tail = sizes
    spans = [(k3, v3, 0, tail), (k2, v2, tail, tok), (k1, v1, tail + tok, tok), (k0, v0, tail + 2 * tok, tok)]
    span = tail + 2 * tok
    rows = LANES
    for step in range(tok // rows):
        first = step * rows
        low, high = first, first + span + rows
        queries = stack_heads(q_ref[first : first + rows, :] * bf16(score_scale))
        starts = cs_ref[first : first + rows, :]
        starts = jnp.concatenate([starts, starts], axis=0)
        parts = []
        for key_ref, value_ref, base, length in spans:
            begin, end = max(low, base), min(high, base + length)
            if begin >= end:
                continue
            keys = key_ref[begin - base : end - base, :]
            scores = mm(queries, keys, NT)
            column = lax.broadcasted_iota(jnp.int32, scores.shape, 1) + begin
            allowed = column >= starts
            if base + length > span:
                row = lax.broadcasted_iota(jnp.int32, scores.shape, 0)
                row = jnp.where(row >= rows, row - rows, row) + (first + span)
                allowed = allowed & (column <= row)
            scores = jnp.where(allowed, scores, masked_fill)
            parts.append((scores, value_ref, begin - base, end - base))
        top = functools.reduce(
            jnp.maximum, [jnp.max(part[0], axis=1, keepdims=True) for part in parts]
        )
        total = jnp.zeros_like(top)
        acc = jnp.zeros((2 * rows, LANES), f32)
        for scores, value_ref, begin, end in parts:
            expanded = jnp.exp(scores - top)
            total = total + jnp.sum(expanded, axis=1, keepdims=True)
            acc = acc + mm(expanded.astype(bf16), value_ref[begin:end, :])
        o_ref[first : first + rows, :] = unstack_heads(acc / total).astype(bf16)
        log_total = top + jnp.log(total)
        lse_ref[first : first + rows, :] = jnp.concatenate(
            [log_total[:rows], log_total[rows:]], axis=1
        )


def self_forward(projected, pieces, starts_col):
    tok, width = projected.shape[1:]
    tail = pieces[2].shape[1]
    pairs = width // LANES

    def spec(part, length):
        return pl.BlockSpec((None, length, LANES), lambda pair, part=part: (part, 0, pair))

    in_specs = [pl.BlockSpec((tok, 1), lambda pair: (0, 0)), spec(0, tok), spec(1, tok), spec(2, tok)]
    operands = [starts_col, projected, projected, projected]
    for piece in pieces:
        in_specs += [spec(0, piece.shape[1]), spec(1, piece.shape[1])]
        operands += [piece, piece]
    area = tok * (tail + 2 * tok + LANES)
    return pl.pallas_call(
        functools.partial(self_forward_kernel, (tok, tail)),
        grid=(pairs,),
        in_specs=in_specs,
        out_specs=[
            pl.BlockSpec((tok, LANES), lambda pair: (0, pair)),
            pl.BlockSpec((None, tok, 2), lambda pair: (pair, 0, 0)),
        ],
        out_shape=[
            jax.ShapeDtypeStruct((tok, width), bf16),
            jax.ShapeDtypeStruct((pairs, tok, 2), f32),
        ],
        compiler_params=pltpu.CompilerParams(vmem_limit_bytes=48 * 1024 * 1024),
        cost_estimate=pl.CostEstimate(
            flops=4 * area * width, bytes_accessed=8 * tok * width * 2, transcendentals=area * 2 * pairs
        ),
        name="self_attention",
    )(*operands)


def self_backward_kernel(
    sizes, cs_ref, lse_ref, delta_ref, q_ref, do_ref, k0, v0, k1, v1, k2, v2, k3, v3,
    dq_ref, d0, d1, d2, d3, dq_acc, q_st, do_st,
):
    tok, tail = sizes
    half = tok // 2
    span = tail + 2 * tok
    lane = lax.broadcasted_iota(jnp.int32, (tok, LANES), 1)
    queries = q_ref[...] * bf16(score_scale)
    grads = do_ref[...]
    zero = jnp.zeros_like(queries)
    q_st[0] = jnp.where(lane < HEAD_DIM, queries, zero)
    q_st[1] = jnp.where(lane < HEAD_DIM, zero, queries)
    do_st[0] = jnp.where(lane < HEAD_DIM, grads, zero)
    do_st[1] = jnp.where(lane < HEAD_DIM, zero, grads)
    dq_acc[...] = jnp.zeros_like(dq_acc)
    blocks = [(k3, v3, d3, 0, 0, tail)]
    for key_ref, value_ref, out_ref, base in ((k2, v2, d2, tail), (k1, v1, d1, tail + tok), (k0, v0, d0, span)):
        blocks += [(key_ref, value_ref, out_ref, base, 0, half), (key_ref, value_ref, out_ref, base, half, half)]
    for key_ref, value_ref, out_ref, base, offset, length in blocks:
        first = base + offset
        q_low = max(0, first - span)
        q_high = min(tok, -(-(first + length) // LANES) * LANES)
        keys = key_ref[offset : offset + length, :]
        values = value_ref[offset : offset + length, :]
        grad_keys = jnp.zeros((length, LANES), f32)
        grad_values = jnp.zeros((length, LANES), f32)
        for head in range(2):
            queries = q_st[head, q_low:q_high, :]
            grads = do_st[head, q_low:q_high, :]
            scores = mm(keys, queries, NT)
            row = lax.broadcasted_iota(jnp.int32, scores.shape, 0) + first
            allowed = row >= cs_ref[:, q_low:q_high]
            if base == span:
                column = lax.broadcasted_iota(jnp.int32, scores.shape, 1) + (q_low + span)
                allowed = allowed & (row <= column)
            probs = jnp.where(allowed, jnp.exp(scores - lse_ref[head : head + 1, q_low:q_high]), 0.0)
            grad_probs = mm(values, grads, NT)
            grad_scores = (probs * (grad_probs - delta_ref[head : head + 1, q_low:q_high])).astype(bf16)
            grad_values = grad_values + mm(probs.astype(bf16), grads)
            grad_keys = grad_keys + mm(grad_scores, queries)
            dq_acc[head, q_low:q_high, :] += mm(grad_scores, keys, TN)
        out_ref[0, offset : offset + length, :] = grad_keys.astype(out_ref.dtype)
        out_ref[1, offset : offset + length, :] = grad_values.astype(out_ref.dtype)
    dq_ref[...] = (jnp.where(lane < HEAD_DIM, dq_acc[0], dq_acc[1]) * score_scale).astype(bf16)


def self_backward(projected, pieces, starts_row, log_total, delta, grad_out):
    tok, width = projected.shape[1:]
    tail = pieces[2].shape[1]
    pairs = width // LANES

    def spec(part, length):
        return pl.BlockSpec((None, length, LANES), lambda pair, part=part: (part, 0, pair))

    def both(length):
        return pl.BlockSpec((2, length, LANES), lambda pair: (0, 0, pair))

    flat = pl.BlockSpec((tok, LANES), lambda pair: (0, pair))
    stat = pl.BlockSpec((None, 2, tok), lambda pair: (pair, 0, 0))
    in_specs = [pl.BlockSpec((1, tok), lambda pair: (0, 0)), stat, stat, spec(0, tok), flat, spec(1, tok), spec(2, tok)]
    operands = [starts_row, log_total, delta, projected, grad_out, projected, projected]
    out_specs = [flat, both(tok)]
    out_shape = [jax.ShapeDtypeStruct((tok, width), bf16), jax.ShapeDtypeStruct((2, tok, width), f32)]
    for piece in pieces:
        in_specs += [spec(0, piece.shape[1]), spec(1, piece.shape[1])]
        operands += [piece, piece]
        out_specs.append(both(piece.shape[1]))
        out_shape.append(jax.ShapeDtypeStruct(piece.shape, bf16))
    area = tok * (tail + 2 * tok + LANES)
    return pl.pallas_call(
        functools.partial(self_backward_kernel, (tok, tail)),
        grid=(pairs,),
        in_specs=in_specs,
        out_specs=out_specs,
        out_shape=out_shape,
        scratch_shapes=[
            pltpu.VMEM((2, tok, LANES), f32),
            pltpu.VMEM((2, tok, LANES), bf16),
            pltpu.VMEM((2, tok, LANES), bf16),
        ],
        compiler_params=pltpu.CompilerParams(vmem_limit_bytes=48 * 1024 * 1024),
        cost_estimate=pl.CostEstimate(
            flops=10 * area * width, bytes_accessed=16 * tok * width * 2, transcendentals=area * 2 * pairs
        ),
        name="self_attention_back",
    )(*operands)


def cross_forward_kernel(ids_ref, slot_ref, q_ref, k_ref, v_ref, o_ref):
    allowed = ids_ref[...] == slot_ref[...]
    for pair in range(q_ref.shape[1] // LANES):
        cols = slice(pair * LANES, (pair + 1) * LANES)
        queries = stack_heads(q_ref[:, cols] * bf16(score_scale))
        scores = mm(queries, k_ref[:, cols], NT)
        rows = scores.shape[0] // 2
        halves = []
        for head in range(2):
            part = jnp.where(allowed, scores[head * rows : (head + 1) * rows], masked_fill)
            expanded = jnp.exp(part - jnp.max(part, axis=1, keepdims=True))
            halves.append(expanded / jnp.sum(expanded, axis=1, keepdims=True))
        probs = jnp.concatenate(halves, axis=0).astype(bf16)
        o_ref[:, cols] = unstack_heads(mm(probs, v_ref[:, cols])).astype(bf16)


def cross_backward_kernel(ids_ref, slot_ref, q_ref, do_ref, k_ref, v_ref, dq_ref, dk_ref, dv_ref):
    allowed = ids_ref[...] == slot_ref[...]
    for pair in range(q_ref.shape[1] // LANES):
        cols = slice(pair * LANES, (pair + 1) * LANES)
        queries = stack_heads(q_ref[:, cols] * bf16(score_scale))
        grads = stack_heads(do_ref[:, cols])
        keys = k_ref[:, cols]
        scores = mm(queries, keys, NT)
        grad_probs = mm(grads, v_ref[:, cols], NT)
        rows = scores.shape[0] // 2
        probs, grad_scores = [], []
        for head in range(2):
            part = jnp.where(allowed, scores[head * rows : (head + 1) * rows], masked_fill)
            expanded = jnp.exp(part - jnp.max(part, axis=1, keepdims=True))
            prob = expanded / jnp.sum(expanded, axis=1, keepdims=True)
            back = grad_probs[head * rows : (head + 1) * rows]
            inner = jnp.sum(prob * back, axis=1, keepdims=True)
            probs.append(prob.astype(bf16))
            grad_scores.append((prob * (back - inner)).astype(bf16))
        probs = jnp.concatenate(probs, axis=0)
        grad_scores = jnp.concatenate(grad_scores, axis=0)
        dq_ref[:, cols] = unstack_heads(mm(grad_scores, keys) * score_scale).astype(bf16)
        dk_ref[:, cols] = mm(grad_scores, queries, TN).astype(dk_ref.dtype)
        dv_ref[:, cols] = mm(probs, grads, TN).astype(dv_ref.dtype)


def cross_call(kernel, outs, ids_col, slot_row, rows, text):
    count, width = rows[0].shape
    keys = text[0].shape[0]
    chunk = width // 3 if width % (3 * LANES) == 0 else width
    row_spec = pl.BlockSpec((count, chunk), lambda group: (0, group))
    text_spec = pl.BlockSpec((keys, chunk), lambda group: (0, group))
    return pl.pallas_call(
        kernel,
        grid=(width // chunk,),
        in_specs=[
            pl.BlockSpec((count, 1), lambda group: (0, 0)),
            pl.BlockSpec((1, keys), lambda group: (0, 0)),
        ]
        + [row_spec] * len(rows)
        + [text_spec] * len(text),
        out_specs=[row_spec if shape.shape[0] == count else text_spec for shape in outs],
        out_shape=outs,
        cost_estimate=pl.CostEstimate(
            flops=4 * len(outs) * count * keys * width,
            bytes_accessed=2 * width * (count + keys) * 3,
            transcendentals=count * keys * width // HEAD_DIM,
        ),
        name="cross_attention" if len(outs) == 1 else "cross_attention_back",
    )(ids_col, slot_row, *rows, *text)


def layer_norm(values, gain_vec, bias_vec):
    center = values - jnp.mean(values, axis=-1, keepdims=True)
    spread = jnp.mean(center * center, axis=-1, keepdims=True)
    return center * lax.rsqrt(spread + norm_eps) * gain_vec + bias_vec


def layer_norm_back(values, gain_vec, grad):
    center = values - jnp.mean(values, axis=-1, keepdims=True)
    spread = jnp.mean(center * center, axis=-1, keepdims=True)
    scale = lax.rsqrt(spread + norm_eps)
    unit = center * scale
    inner = grad * gain_vec
    mean_inner = jnp.mean(inner, axis=-1, keepdims=True)
    mean_cross = jnp.mean(inner * unit, axis=-1, keepdims=True)
    result = scale * (inner - mean_inner - unit * mean_cross)
    return (result, jnp.sum(grad * unit, axis=0), jnp.sum(grad, axis=0))


def local(
    inputs, clip_ids, clip_pos, text_states, norm_gain, norm_bias, self_qkv, self_out,
    cross_q, cross_kv, cross_out, mlp_up, mlp_down, cotangent,
):
    tok_count = clip_ids.shape[0]
    layer_count = norm_gain.shape[0]
    clip_count = text_states.shape[0]
    own_count, model_width = inputs.shape
    dp_count, fs_count, mp_count = (lax.axis_size(name) for name in ("dp", "fsdp", "mp"))
    pairwise = dp_count == 4
    paired = pairwise and fs_count == 2
    dp_index, fs_index, mp_index = (lax.axis_index(name) for name in ("dp", "fsdp", "mp"))
    core, cross_x = dp_index % 2, dp_index // 2
    cell = model_width // 4
    slice_width = self_out.shape[1]
    half_slice = slice_width // 2

    if paired:
        cells = [
            2 * fs_index + core, 2 * (1 - fs_index) + core,
            2 * fs_index + 1 - core, 2 * (1 - fs_index) + 1 - core,
        ]
        places = [
            jnp.where(number // 2 == fs_index, 0, 1) + 2 * jnp.where(number % 2 == core, 0, 1)
            for number in range(4)
        ]

    def pick_cells(values, order):
        if not paired:
            return values
        axis = values.ndim - 1
        return jnp.concatenate([part_of(values, place, cell, axis) for place in order], axis=axis)

    def to_local(values):
        return pick_cells(values, cells if paired else None)

    def to_global(values):
        return pick_cells(values, places if paired else None)

    def spread_rows(values):
        return lax.all_gather(values, "mp", axis=0, tiled=True)

    def reduce_rows(values):
        return lax.psum_scatter(
            values.astype(bf16), "mp", scatter_dimension=0, tiled=True
        ).astype(f32)

    def gather_slice(shard, axis):
        if not paired:
            return lax.all_gather(shard, "fsdp", axis=axis, tiled=True)
        own = part_of(shard, core, cell, axis)
        far = swapped(own, "fsdp", 1)
        return jnp.concatenate(
            [own, far, part_of(shard, 1 - core, cell, axis), swapped(far, "dp", 1)], axis=axis
        )

    def gather_square(shard, axis):
        heads = 1 - axis
        if not paired:
            whole = lax.all_gather(shard, "fsdp", axis=axis, tiled=True)
            return lax.all_gather(whole, "mp", axis=heads, tiled=True)
        part = part_of(part_of(shard, core, cell, axis), cross_x, half_slice, heads)
        part = lax.all_gather(part, "mp", axis=0, tiled=False)
        part = jnp.concatenate([part, swapped(part, "fsdp", 1)], axis=axis + 1)
        part = jnp.expand_dims(part, heads + 1)
        part = ordered(cross_x, part, swapped(part, "dp", 2), heads + 1)
        if heads == 0:
            part = part.reshape(mp_count * slice_width, 2 * cell)
        else:
            part = part.reshape(mp_count, 2 * cell, slice_width)
            part = part.transpose(1, 0, 2).reshape(2 * cell, mp_count * slice_width)
        return jnp.concatenate([part, swapped(part, "dp", 1)], axis=axis)

    def sum_narrow(own, other):
        return (own.astype(f32) + other.astype(f32)).astype(bf16)

    def reduce_over_replicas(value, axis):
        value = value.astype(bf16)
        if paired:
            keep = lax.slice_in_dim(value, 0, 2 * cell, axis=axis)
            value = sum_narrow(keep, swapped(lax.slice_in_dim(value, 2 * cell, 4 * cell, axis=axis), "dp", 1))
            keep = lax.slice_in_dim(value, 0, cell, axis=axis)
            return sum_narrow(keep, swapped(lax.slice_in_dim(value, cell, 2 * cell, axis=axis), "fsdp", 1))
        return lax.psum_scatter(value, "fsdp", scatter_dimension=axis, tiled=True)

    def reduce_slice(value, axis):
        value = reduce_over_replicas(value, axis)
        if not paired:
            return lax.psum(value, "dp").astype(f32)
        value = sum_narrow(value, swapped(value, "dp", 2))
        return ordered(core, value, swapped(value, "dp", 1), axis).astype(f32)

    def reduce_square(value, axis):
        heads = 1 - axis
        if not paired:
            value = reduce_over_replicas(value, axis)
            value = lax.psum_scatter(value, "mp", scatter_dimension=heads, tiled=True)
            return lax.psum(value, "dp").astype(f32)
        value = reduce_over_replicas(value, axis)
        shape = value.shape[:heads] + (mp_count, 2, half_slice) + value.shape[heads + 1 :]
        value = value.reshape(shape)
        sent = swapped(part_of(value, 1 - cross_x, 1, heads + 1), "dp", 2)
        value = sum_narrow(part_of(value, cross_x, 1, heads + 1), sent)
        value = lax.psum_scatter(value, "mp", scatter_dimension=heads, tiled=True)
        value = jnp.squeeze(value, (heads, heads + 1))
        value = ordered(cross_x, value, swapped(value, "dp", 2), heads)
        return ordered(core, value, swapped(value, "dp", 1), axis).astype(f32)

    def sum_everywhere(value, axes):
        for axis in axes:
            count = lax.axis_size(axis)
            if count in (2, 4):
                mask = 1
                while mask < count:
                    value = value + swapped(value, axis, mask)
                    mask *= 2
            else:
                value = lax.psum(value, axis)
        return value

    group_base = lax.axis_index(("dp", "fsdp")) * tok_count
    tail = CLIP_HI - 2 * tok_count
    clip_start = (
        jnp.arange(tok_count, dtype=jnp.int32) + (tail + 2 * tok_count) - clip_pos
    )
    starts_col, starts_row = clip_start[:, None], clip_start[None, :]
    slot_first = jnp.minimum(clip_ids[0], clip_count - SLOTS)
    slot_row = (slot_first + jnp.arange(SLOTS * TEXT, dtype=jnp.int32) // TEXT)[None, :]
    ids_col = part_of(clip_ids, mp_index, own_count, 0)[:, None]
    text_rows = to_local(
        lax.dynamic_slice_in_dim(text_states, slot_first, SLOTS, 0).reshape(SLOTS * TEXT, model_width)
    )
    norms = jnp.concatenate([norm_gain, norm_bias], axis=1)
    norms = to_local(lax.all_gather(norms, "fsdp", axis=2, tiled=True)).astype(f32)
    gains, biases = norms[:, :3], norms[:, 3:]

    residual = to_local(inputs).astype(f32)
    saved = []
    for layer in range(layer_count):
        w_qkv = gather_slice(self_qkv[layer], 0)
        w_kv = gather_slice(cross_kv[layer], 0)
        w_so = gather_square(self_out[layer], 1)
        w_cq = gather_square(cross_q[layer], 0)
        w_co = gather_square(cross_out[layer], 1)
        w_up = gather_slice(mlp_up[layer], 0)
        w_down = gather_slice(mlp_down[layer], 1)

        start_res = residual
        normed = layer_norm(residual, gains[layer, 0], biases[layer, 0]).astype(bf16)
        rows_one = spread_rows(normed)
        projected = jnp.einsum("td,dcj->ctj", rows_one, w_qkv, preferred_element_type=f32).astype(bf16)
        key_values = projected[1:]
        pieces = [
            passed_along(key_values, ("dp", "fsdp"), 1),
            passed_along(key_values, ("dp", "fsdp"), 2),
            passed_along(key_values[:, tok_count - tail :], ("dp", "fsdp"), 3),
        ]
        heads_out, log_self = self_forward(projected, pieces, starts_col)
        merged_one = lax.all_to_all(heads_out, "mp", split_axis=0, concat_axis=1, tiled=True)
        residual = residual + mm(merged_one, w_so)
        mid_res = residual
        normed_two = layer_norm(residual, gains[layer, 1], biases[layer, 1]).astype(bf16)
        cross_query = mm(normed_two, w_cq).astype(bf16)
        text_kv = jnp.einsum("sd,dcj->csj", text_rows, w_kv, preferred_element_type=f32).astype(bf16)
        text_kv = lax.all_gather(text_kv, "mp", axis=2, tiled=True)
        text_k, text_v = text_kv[0], text_kv[1]
        (merged_two,) = cross_call(
            cross_forward_kernel,
            [jax.ShapeDtypeStruct((own_count, model_width), bf16)],
            ids_col, slot_row, [cross_query], [text_k, text_v],
        )
        residual = residual + mm(merged_two, w_co)
        late_res = residual
        normed = layer_norm(residual, gains[layer, 2], biases[layer, 2]).astype(bf16)
        rows_three = spread_rows(normed)
        upward = mm(rows_three, w_up)
        activated = jax.nn.gelu(upward).astype(bf16)
        residual = residual + reduce_rows(mm(activated, w_down))
        saved.append(
            (
                (w_qkv, w_kv, w_so, w_cq, w_co, w_up, w_down),
                start_res, mid_res, late_res, rows_one, projected, pieces, heads_out, log_self,
                merged_one, normed_two, cross_query, text_k, text_v, merged_two, rows_three,
                upward, activated,
            )
        )
    output = to_global(residual.astype(bf16))

    grad_res = to_local(cotangent).astype(f32)
    text_acc = jnp.zeros((SLOTS * TEXT, model_width), f32)
    matrix_list, gain_list, bias_list = [], [], []
    for layer in reversed(range(layer_count)):
        (
            (w_qkv, w_kv, w_so, w_cq, w_co, w_up, w_down),
            start_res, mid_res, late_res, rows_one, projected, pieces, heads_out, log_self,
            merged_one, normed_two, cross_query, text_k, text_v, merged_two, rows_three,
            upward, activated,
        ) = saved[layer]
        grad_full = spread_rows(grad_res.astype(bf16))
        grad_act = mm(grad_full, w_down, NT)
        grad_up_rows = jax.vjp(jax.nn.gelu, upward)[1](grad_act)[0].astype(bf16)
        grad_normed = reduce_rows(mm(grad_up_rows, w_up, NT))
        grad_down = reduce_slice(mm(activated, grad_full, TN), 1)
        grad_up = reduce_slice(mm(rows_three, grad_up_rows, TN), 0)
        res_part, gain_three, bias_three = layer_norm_back(late_res, gains[layer, 2], grad_normed)
        grad_res = grad_res + res_part
        narrow = grad_res.astype(bf16)
        grad_merged = mm(narrow, w_co, NT).astype(bf16)
        grad_cq_rows, grad_tk, grad_tv = cross_call(
            cross_backward_kernel,
            [
                jax.ShapeDtypeStruct((own_count, model_width), bf16),
                jax.ShapeDtypeStruct((SLOTS * TEXT, model_width), bf16),
                jax.ShapeDtypeStruct((SLOTS * TEXT, model_width), bf16),
            ],
            ids_col, slot_row, [cross_query, grad_merged], [text_k, text_v],
        )
        grad_co = reduce_square(mm(merged_two, narrow, TN), 1)
        grad_cq = reduce_square(mm(normed_two, grad_cq_rows, TN), 0)
        grad_normed = mm(grad_cq_rows, w_cq, NT)
        res_part, gain_two, bias_two = layer_norm_back(mid_res, gains[layer, 1], grad_normed)
        grad_res = grad_res + res_part
        narrow = grad_res.astype(bf16)
        grad_merged = mm(narrow, w_so, NT).astype(bf16)
        grad_heads = lax.all_to_all(grad_merged, "mp", split_axis=1, concat_axis=0, tiled=True)
        grad_so = reduce_square(mm(merged_one, narrow, TN), 1)
        grad_text_kv = lax.psum_scatter(
            jnp.stack([grad_tk, grad_tv]), "mp", scatter_dimension=2, tiled=True
        )
        grad_kv = reduce_slice(
            jnp.einsum("sd,csj->dcj", text_rows, grad_text_kv, preferred_element_type=f32), 0
        )
        text_acc = text_acc + jnp.einsum(
            "csj,dcj->sd", grad_text_kv, w_kv, preferred_element_type=f32
        )
        pairs = heads_out.shape[1] // LANES
        delta = (grad_heads.astype(f32) * heads_out.astype(f32)).reshape(tok_count, 2 * pairs, HEAD_DIM)
        delta = jnp.sum(delta, axis=2).T.reshape(pairs, 2, tok_count)
        grad_q, own_kv, *far_kv = self_backward(
            projected, pieces, starts_row, log_self.transpose(0, 2, 1), delta, grad_heads
        )
        own_kv = own_kv + passed_along(far_kv[0], ("dp", "fsdp"), -1).astype(f32)
        own_kv = own_kv + passed_along(far_kv[1], ("dp", "fsdp"), -2).astype(f32)
        far_tail = passed_along(far_kv[2], ("dp", "fsdp"), -3).astype(f32)
        own_kv = own_kv + jnp.pad(far_tail, ((0, 0), (tok_count - tail, 0), (0, 0)))
        grad_proj = jnp.concatenate([grad_q[None], own_kv.astype(bf16)], axis=0)
        grad_normed = reduce_rows(
            jnp.einsum("ctj,dcj->td", grad_proj, w_qkv, preferred_element_type=f32)
        )
        grad_qkv = reduce_slice(
            jnp.einsum("td,ctj->dcj", rows_one, grad_proj, preferred_element_type=f32), 0
        )
        res_part, gain_one, bias_one = layer_norm_back(start_res, gains[layer, 0], grad_normed)
        grad_res = grad_res + res_part
        gain_list.insert(0, jnp.stack([gain_one, gain_two, gain_three]))
        bias_list.insert(0, jnp.stack([bias_one, bias_two, bias_three]))
        matrix_list.insert(0, (grad_qkv, grad_so, grad_cq, grad_kv, grad_co, grad_up, grad_down))

    stacked = [jnp.stack([layer_set[member] for layer_set in matrix_list]) for member in range(7)]
    norm_grads = to_global(jnp.stack([jnp.stack(gain_list), jnp.stack(bias_list)]))
    norm_grads = sum_everywhere(norm_grads, ("mp", "dp", "fsdp"))
    norm_grads = part_of(norm_grads, fs_index, model_width // fs_count, 3)

    text_full = jnp.zeros((clip_count, TEXT, model_width), f32)
    text_full = lax.dynamic_update_slice_in_dim(
        text_full, to_global(text_acc).reshape(SLOTS, TEXT, model_width), slot_first, 0
    )
    text_grad = lax.psum(text_full, ("dp", "fsdp", "mp"))
    return (output, to_global(grad_res), text_grad, norm_grads[0], norm_grads[1], *stacked)


def solution(mesh):
    in_specs = (
        P(("dp", "fsdp", "mp"), None),
        P(("dp", "fsdp")),
        P(("dp", "fsdp")),
        P(),
        P(None, None, "fsdp"),
        P(None, None, "fsdp"),
        P(None, "fsdp", None, "mp"),
        P(None, "mp", "fsdp"),
        P(None, "fsdp", "mp"),
        P(None, "fsdp", None, "mp"),
        P(None, "mp", "fsdp"),
        P(None, "fsdp", "mp"),
        P(None, "mp", "fsdp"),
        P(("dp", "fsdp", "mp"), None),
    )
    out_specs = (
        P(("dp", "fsdp", "mp"), None),
        P(("dp", "fsdp", "mp"), None),
        P(),
        P(None, None, "fsdp"),
        P(None, None, "fsdp"),
        P(None, "fsdp", None, "mp"),
        P(None, "mp", "fsdp"),
        P(None, "fsdp", "mp"),
        P(None, "fsdp", None, "mp"),
        P(None, "mp", "fsdp"),
        P(None, "fsdp", "mp"),
        P(None, "mp", "fsdp"),
    )
    return jax.shard_map(local, mesh=mesh, in_specs=in_specs, out_specs=out_specs, check_vma=False)
```

time: 3500 us -> 1620 us (0.46)
  waiting for transfers between devices: 2520 us -> 578 us
  matrix products: 518 us -> 189 us
  Pallas kernels: 0 us -> 115 us
  blocking collectives: 81.4 us -> 194 us
  other arithmetic: 112 us -> 199 us
  starting transfers between devices: 43 us -> 129 us
    reduce_scatter x26 -> x12, waiting for transfers between devices: 971 us -> 54.8 us  [the longest x6 54.8 us: reduce_rows(): lax.psum_scatter(values.astype(bf16), 'mp', scatter_dimension=0, tiled=True)]
    all_gather x20 -> x0, waiting for transfers between devices: 709 us -> none  [the longest x6 250 us: gather_grads(): return lax.all_gather(values, 'mp', axis=0, tiled=True)]
    ppermute x0 -> x101, waiting for transfers between devices: none -> 414 us  [swapped(): lax.ppermute(value, axis, [(source, source ^ mask) for source in range(co...]
    dot_general x208 -> x40, matrix products: 514 us -> 187 us  [the longest x30 147 us: mm(): return lax.dot_general(a, b, dims, preferred_element_type=f32)]
    psum x1 -> x0, waiting for transfers between devices: 268 us -> none  [local(): lax.psum(shares[2].astype(jnp.bfloat16), 'dp').astype(jnp.float32)]
    all_gather x6, waiting for transfers between devices: 268 us -> 51.7 us  [spread_rows(): return lax.all_gather(values, 'mp', axis=0, tiled=True)]
    all_gather x4 -> x9, blocking collectives: 18.4 us -> 194 us  [the longest x6 121 us: gather_square(): part = lax.all_gather(part, 'mp', axis=0, tiled=False)]
    pallas_call x0 -> x8, Pallas kernels: none -> 115 us  [the longest x2 60.8 us: self_backward(): pl.pallas_call(functools.partial(self_backward_kernel, (tok, tail)), grid...]
  transfers between devices with their start and end apart: 70 -> 138, of which waited for: 63 -> 48; matrix products, arithmetic and copies ran while one was open for 10% -> 31% of each run, Pallas kernels for 0% -> 7%
where the time goes in v1:
time: 1620 us; the launch traced here: 1610 us
  waiting for transfers between devices  578 us (36%)
  other arithmetic  199 us (12%)
  blocking collectives  194 us (12%)
  local copies, waits for them, and re-layouts  191 us (12%)
  matrix products  189 us (12%)
  starting transfers between devices  129 us (8%)
  Pallas kernels  115 us (7%)
  between operations  18.7 us (1%)
    ppermute x101, waiting for transfers between devices, swapped(): lax.ppermute(value, axis, [(source, source ^ mask) for source in range(co...  414 us
    dot_general x30, matrix products, mm(): return lax.dot_general(a, b, dims, preferred_element_type=f32)  147 us
    all_gather x6, blocking collectives, gather_square(): part = lax.all_gather(part, 'mp', axis=0, tiled=False)  121 us
    ppermute x101, starting transfers between devices, swapped(): lax.ppermute(value, axis, [(source, source ^ mask) for source in range(co...  87.8 us
    convert_element_type x42, other arithmetic, sum_narrow(): return (own.astype(f32) + other.astype(f32)).astype(bf16)  79.3 us
    unnamed x481, local copies, waits for them, and re-layouts  65.4 us
    pallas_call x2, Pallas kernels, self_backward(): pl.pallas_call(functools.partial(self_backward_kernel, (tok, tail)), grid...  60.8 us
    all_gather x2, blocking collectives, local(): text_kv = lax.all_gather(text_kv, 'mp', axis=2, tiled=True)  56.6 us
  transfers between devices with their start and end apart: 138, of which 48 were waited for; matrix products, arithmetic and copies ran while one was open for 31% of the time, Pallas kernels for 7%

profile of v1, /device:TPU:0, one launch (start us, length us, event | category | flops | bytes accessed | tf_op | source)
XLA Modules:
  0.0 1614.8 jit_solution(5871068119064627074)
XLA Ops:
  9.7 18.2 %all_gather.56 = bf16[4,192,384]{2,1,0:T(8,128)(2,1)S(1)} all-gather(bf16[1,192,384]{2,1,0:T(8,128)(2,1)S(1)} %constant_dynamic-slice_fusion.31), channel_id=1, replica_groups=mesh['dp'=4,'fsdp'=2,'mp'=4] {'mp'}, dimensions={0}, use_global_device_ids=true | all-gather | bytes 737280 | tf_op jit(solution)/shard_map/all_gather | solution.py:381
  30.5 17.0 %all_gather.53 = bf16[4,192,384]{2,1,0:T(8,128)(2,1)} all-gather(bf16[1,192,384]{2,1,0:T(8,128)(2,1)S(1)} %constant_dynamic-slice_fusion.40), channel_id=1, replica_groups=mesh['dp'=4,'fsdp'=2,'mp'=4] {'mp'}, dimensions={0}, use_global_device_ids=true | all-gather | bytes 737280 | tf_op jit(solution)/shard_map/all_gather | solution.py:381
  60.4 16.6 %all_gather.51 = bf16[2,6,1536]{2,0,1:T(2,128)(2,1)S(1)} all-gather(bf16[2,6,768]{2,0,1:T(2,128)(2,1)S(1)} %pad_maximum_fusion.96), channel_id=1, replica_groups=mesh['dp'=4,'fsdp'=2,'mp'=4] {'fsdp'}, dimensions={2}, use_global_device_ids=true | all-gather | bytes 55296 | tf_op jit(solution)/shard_map/all_gather | solution.py:452
  80.2 19.6 %all_gather.60 = bf16[4,384,192]{1,2,0:T(8,128)(2,1)S(1)} all-gather(bf16[1,384,192]{1,2,0:T(8,128)(2,1)S(1)} %copy.200), channel_id=1, replica_groups=mesh['dp'=4,'fsdp'=2,'mp'=4] {'mp'}, dimensions={0}, use_global_device_ids=true | all-gather | bytes 737280 | tf_op jit(solution)/shard_map/all_gather | solution.py:381
  101.0 22.7 %all_gather.54 = bf16[4,384,192]{1,2,0:T(8,128)(2,1)S(1)} all-gather(bf16[1,384,192]{1,2,0:T(8,128)(2,1)S(1)} %copy.198), channel_id=1, replica_groups=mesh['dp'=4,'fsdp'=2,'mp'=4] {'mp'}, dimensions={0}, use_global_device_ids=true | all-gather | bytes 737280 | tf_op jit(solution)/shard_map/all_gather | solution.py:381
  157.0 25.3 %collective-permute-done.6 = bf16[4,1,192,768]{3,2,1,0:T(8,128)(2,1)} collective-permute-done((bf16[4,1,192,768]{3,2,1,0:T(8,128)(2,1)}, bf16[4,1,192,768]{3,2,1,0:T(8,128)(2,1)}, u32[]{:S(2)}, u32[]{:S(2)}) %collective-permute-start.6) | collective-permute-done | bytes 1179680 | tf_op jit(solution)/shard_map/ppermute | solution.py:41
  195.8 11.8 collective-permute-done.29
  208.9 22.8 %collective-permute-done.9 = bf16[4,768,1,192]{1,3,2,0:T(8,128)(2,1)} collective-permute-done((bf16[4,768,1,192]{1,3,2,0:T(8,128)(2,1)}, bf16[4,768,1,192]{1,3,2,0:T(8,128)(2,1)}, u32[]{:S(2)}, u32[]{:S(2)}) %collective-permute-start.9) | collective-permute-done | bytes 1179680 | tf_op jit(solution)/shard_map/ppermute | solution.py:41
  247.2 13.2 self_attention.2
  264.5 27.9 %all_gather.55 = bf16[2,128,1536]{2,1,0:T(8,128)(2,1)S(1)} all-gather(bf16[2,128,384]{2,1,0:T(8,128)(2,1)S(1)} %copy-done.166), channel_id=1, replica_groups=mesh['dp'=4,'fsdp'=2,'mp'=4] {'mp'}, dimensions={2}, use_global_device_ids=true | all-gather | bytes 983040 | tf_op jit(solution)/shard_map/all_gather | solution.py:483
  318.7 6.5 collective-permute-start.16
  331.5 20.6 %collective-permute-done.16 = bf16[384,1536]{1,0:T(8,128)(2,1)S(1)} collective-permute-done((bf16[384,1536]{1,0:T(8,128)(2,1)S(1)}, bf16[384,1536]{1,0:T(8,128)(2,1)S(1)}, u32[]{:S(2)}, u32[]{:S(2)}) %collective-permute-start.16) | collective-permute-done | bytes 1179680 | tf_op jit(solution)/shard_map/ppermute | solution.py:41
  352.1 22.3 %collective-permute-done.18 = bf16[1536,384]{1,0:T(8,128)(2,1)} collective-permute-done((bf16[1536,384]{1,0:T(8,128)(2,1)S(1)}, bf16[1536,384]{1,0:T(8,128)(2,1)}, u32[]{:S(2)}, u32[]{:S(2)}) %collective-permute-start.18) | collective-permute-done | bytes 1179680 | tf_op jit(solution)/shard_map/ppermute | solution.py:41
  374.5 5.7 fusion.99
  382.2 6.4 convolution_convert_fusion.17
  389.7 40.7 %reduce-scatter.19.cloned.1.call-done = bf16[160,1536]{1,0:T(8,128)(2,1)} async-done(((bf16[640,1536]{1,0:T(8,128)(2,1)}), bf16[160,1536]{1,0:T(8,128)(2,1)}) %reduce-scatter.19.cloned.1.call-update) | async-done | bytes 491536 | tf_op jit(solution)/shard_map/reduce_scatter | solution.py:362
  433.3 19.9 %all_gather.59 = bf16[4,192,384]{2,1,0:T(8,128)(2,1)S(1)} all-gather(bf16[1,192,384]{2,1,0:T(8,128)(2,1)S(1)} %constant_dynamic-slice_fusion.28), channel_id=1, replica_groups=mesh['dp'=4,'fsdp'=2,'mp'=4] {'mp'}, dimensions={0}, use_global_device_ids=true | all-gather | bytes 737280 | tf_op jit(solution)/shard_map/all_gather | solution.py:381
  455.1 23.7 %all_gather.62 = bf16[4,192,384]{2,1,0:T(8,128)(2,1)S(1)} all-gather(bf16[1,192,384]{2,1,0:T(8,128)(2,1)S(1)} %constant_dynamic-slice_fusion.24), channel_id=1, replica_groups=mesh['dp'=4,'fsdp'=2,'mp'=4] {'mp'}, dimensions={0}, use_global_device_ids=true | all-gather | bytes 737280 | tf_op jit(solution)/shard_map/all_gather | solution.py:381
  482.0 6.7 collective-permute-done.33
  498.6 16.2 %collective-permute-done.20 = bf16[384,3,384]{0,2,1:T(8,128)(2,1)} collective-permute-done((bf16[384,3,384]{0,2,1:T(8,128)(2,1)}, bf16[384,3,384]{0,2,1:T(8,128)(2,1)}, u32[]{:S(2)}, u32[]{:S(2)}) %collective-permute-start.20) | collective-permute-done | bytes 884768 | tf_op jit(solution)/shard_map/ppermute | solution.py:41
  521.2 7.5 collective-permute-done.34
  534.6 5.4 fusion.49.q_ref.k0.v0
  558.6 11.4 collective-permute-done.24.k3.v3
  572.8 13.7 self_attention.3
  592.5 28.7 %all_gather.61 = bf16[2,128,1536]{2,1,0:T(8,128)(2,1)S(1)} all-gather(bf16[2,128,384]{2,1,0:T(8,128)(2,1)} %fusion.72), channel_id=1, replica_groups=mesh['dp'=4,'fsdp'=2,'mp'=4] {'mp'}, dimensions={2}, use_global_device_ids=true | all-gather | bytes 983040 | tf_op jit(solution)/shard_map/all_gather | solution.py:483
  655.8 21.8 %collective-permute-done.36 = bf16[384,1536]{1,0:T(8,128)(2,1)} collective-permute-done((bf16[384,1536]{1,0:T(8,128)(2,1)}, bf16[384,1536]{1,0:T(8,128)(2,1)}, u32[]{:S(2)}, u32[]{:S(2)}) %collective-permute-start.36) | collective-permute-done | bytes 1179680 | tf_op jit(solution)/shard_map/ppermute | solution.py:41
  677.6 21.8 %collective-permute-done.38 = bf16[1536,384]{1,0:T(8,128)(2,1)} collective-permute-done((bf16[1536,384]{1,0:T(8,128)(2,1)S(1)}, bf16[1536,384]{1,0:T(8,128)(2,1)}, u32[]{:S(2)}, u32[]{:S(2)}) %collective-permute-start.38) | collective-permute-done | bytes 1179680 | tf_op jit(solution)/shard_map/ppermute | solution.py:41
  699.4 8.0 fusion.97
  707.5 29.2 %all-gather.15.cloned.1.call-done = bf16[640,1536]{1,0:T(8,128)(2,1)} async-done(((bf16[160,1536]{1,0:T(8,128)(2,1)}), bf16[640,1536]{1,0:T(8,128)(2,1)}) %all-gather.15.cloned.1.call-update) | async-done | bytes 1966096 | tf_op jit(solution)/shard_map/all_gather | solution.py:359
  736.6 8.0 fusion.13
  746.0 6.5 convolution_convert_fusion.15
  752.5 6.7 convolution_convert_fusion
  772.9 6.4 convolution_convert_fusion.16
  790.6 22.4 %collective-permute-done.110 = bf16[1536,384]{0,1:T(8,128)(2,1)} collective-permute-done((bf16[1536,384]{0,1:T(8,128)(2,1)}, bf16[1536,384]{0,1:T(8,128)(2,1)}, u32[]{:S(2)}, u32[]{:S(2)}) %collective-permute-start.110) | collective-permute-done | bytes 1179680 | tf_op jit(solution)/shard_map/ppermute | solution.py:41
  817.4 19.6 %collective-permute-done.102 = bf16[384,1536]{1,0:T(8,128)(2,1)} collective-permute-done((bf16[384,1536]{1,0:T(8,128)(2,1)}, bf16[384,1536]{1,0:T(8,128)(2,1)}, u32[]{:S(2)}, u32[]{:S(2)}) %collective-permute-start.102) | collective-permute-done | bytes 1179680 | tf_op jit(solution)/shard_map/ppermute | solution.py:41
  846.5 8.9 cross_attention_back.2
  855.4 5.2 multiply_reduce_fusion
  886.8 30.5 %self_attention_back.2 = (bf16[640,384]{1,0:T(8,128)(2,1)S(1)}, f32[2,640,384]{2,1,0:T(8,128)}, bf16[2,640,384]{2,1,0:T(8,128)(2,1)S(1)}, bf16[2,640,384]{2,1,0:T(8,128)(2,1)S(1)}, bf16[2,256,384]{2,1,0:T(8,128)(2,1)S(1)}) custom-call(s32[1,640]{1,0:T(1,128)S(1)} %broadcast_in_dim.32.cs_ref, f32[3,2,640]{2,1,0:T(2,128)S(1)} %bitcast.297, ...), custom_call_target="tpu_custom_call" | custom-call | flops 4089446400 | bytes 7864320 | tf_op jit(solution)/shard_map/self_attention_back/pallas_call | solution.py:214
  942.9 8.9 collective-permute-done.42
  956.4 5.4 bitcast_convert_fusion.1
  967.9 10.4 collective-permute-done.103
  989.5 5.6 collective-permute-done.93
  1005.0 15.3 collective-permute-done.75
  1030.0 15.0 collective-permute-done.65
  1088.1 8.6 collective-permute-done.85
  1105.6 15.2 collective-permute-done.57
  1124.7 22.5 %all-gather.17.cloned.1.call-done = bf16[640,1536]{1,0:T(8,128)(2,1)} async-done(((bf16[160,1536]{1,0:T(8,128)(2,1)}), bf16[640,1536]{1,0:T(8,128)(2,1)}) %all-gather.17.cloned.1.call-update) | async-done | bytes 1966096 | tf_op jit(solution)/shard_map/all_gather | solution.py:359
  1147.1 8.1 fusion.6
  1156.5 5.8 convolution_convert_fusion.14
  1162.9 6.7 convolution_convert_fusion.1
  1188.7 14.1 reduce-scatter.27.cloned.1.call-done
  1216.2 8.9 cross_attention_back.3
  1264.0 12.9 collective-permute-done.88
  1308.6 18.8 %collective-permute-done.60 = bf16[1536,384]{1,0:T(8,128)(2,1)} collective-permute-done((bf16[1536,384]{1,0:T(8,128)(2,1)}, bf16[1536,384]{1,0:T(8,128)(2,1)}, u32[]{:S(2)}, u32[]{:S(2)}) %collective-permute-start.60) | collective-permute-done | bytes 1179680 | tf_op jit(solution)/shard_map/ppermute | solution.py:41
  1337.2 30.2 %self_attention_back.3 = (bf16[640,384]{1,0:T(8,128)(2,1)S(1)}, f32[2,640,384]{2,1,0:T(8,128)}, bf16[2,640,384]{2,1,0:T(8,128)(2,1)}, bf16[2,640,384]{2,1,0:T(8,128)(2,1)}, bf16[2,256,384]{2,1,0:T(8,128)(2,1)S(1)}) custom-call(s32[1,640]{1,0:T(1,128)S(1)} %broadcast_in_dim.32.cs_ref, f32[3,2,640]{2,1,0:T(2,128)S(1)} %bitcast.296, ...), custom_call_target="tpu_custom_call" | custom-call | flops 4089446400 | bytes 7864320 | tf_op jit(solution)/shard_map/self_attention_back/pallas_call | solution.py:214
  1383.0 17.4 %collective-permute-done.45 = bf16[2,256,384]{2,1,0:T(8,128)(2,1)S(1)} collective-permute-done((bf16[2,256,384]{2,1,0:T(8,128)(2,1)S(1)}, bf16[2,256,384]{2,1,0:T(8,128)(2,1)S(1)}, u32[]{:S(2)}, u32[]{:S(2)}) %collective-permute-start.45) | collective-permute-done | bytes 393248 | tf_op jit(solution)/shard_map/ppermute | solution.py:36
  1404.6 5.8 bitcast_convert_fusion
  1419.7 9.8 collective-permute-done.107
  1432.5 21.8 %collective-permute-done.99 = bf16[384,1536]{1,0:T(8,128)(2,1)S(1)} collective-permute-done((bf16[384,1536]{1,0:T(8,128)(2,1)}, bf16[384,1536]{1,0:T(8,128)(2,1)S(1)}, u32[]{:S(2)}, u32[]{:S(2)}) %collective-permute-start.99) | collective-permute-done | bytes 1179680 | tf_op jit(solution)/shard_map/ppermute | solution.py:41
  1485.4 9.8 copy.180
  1500.8 14.0 collective-permute-done.81
  1526.2 5.8 copy.179
  1533.8 8.9 collective-permute-done.53
  1586.7 18.4 %all-reduce.4.cloned.1.call-done = f32[4,64,1536]{2,1,0:T(8,128)} async-done(((f32[4,64,1536]{2,1,0:T(8,128)}), f32[4,64,1536]{2,1,0:T(8,128)}) %all-reduce.4.cloned.1.call-update) | async-done | bytes 1572880 | tf_op jit(solution)/shard_map/psum | solution.py:586
  (1051 shorter events, 646.4 us)
Async XLA Ops:
  7.2 181.1 %all-gather.7.cloned.1.call-start = ((), (), s32[]{:S(2)}) async-start(), calls=%async_computation.18 | async-start | bytes 2457600 | tf_op jit(solution)/shard_map/all_gather | solution.py:359
  27.9 97.8 %collective-permute-start.13 = (bf16[4,192,384]{2,1,0:T(8,128)(2,1)S(1)}, bf16[4,192,384]{2,1,0:T(8,128)(2,1)}, u32[]{:S(2)}, u32[]{:S(2)}) collective-permute-start(bf16[4,192,384]{2,1,0:T(8,128)(2,1)S(1)} %all_gather.56), channel_id=1, source_target_pairs={{0,4},{4,0},{1,5},{5,1},{2,6},{6,2},{3,7},{7,3},{8,12},{12,8},{9,1... | collective-permute-start | bytes 1769480 | tf_op jit(solution)/shard_map/ppermute | solution.py:41
  47.5 81.7 %collective-permute-start.5 = (bf16[4,192,384]{2,1,0:T(8,128)(2,1)}, bf16[4,192,384]{2,1,0:T(8,128)(2,1)}, u32[]{:S(2)}, u32[]{:S(2)}) collective-permute-start(bf16[4,192,384]{2,1,0:T(8,128)(2,1)} %all_gather.53), channel_id=1, source_target_pairs={{0,4},{4,0},{1,5},{5,1},{2,6},{6,2},{3,7},{7,3},{8,12},{12,8},{9,1... | collective-permute-start | bytes 1769480 | tf_op jit(solution)/shard_map/ppermute | solution.py:41
  57.1 85.4 %collective-permute-start = (bf16[384,3,384]{0,2,1:T(8,128)(2,1)}, bf16[384,3,384]{0,2,1:T(8,128)(2,1)}, u32[]{:S(2)}, u32[]{:S(2)}) collective-permute-start(bf16[384,3,384]{0,2,1:T(8,128)(2,1)} %bitcast.330), channel_id=1, source_target_pairs={{0,4},{4,0},{1,5},{5,1},{2,6},{6,2},{3,7},{7,3},{8,12},{12,8},{9,1... | collective-permute-start | bytes 2654216 | tf_op jit(solution)/shard_map/ppermute | solution.py:41
  99.7 42.5 %collective-permute-start.28 = (bf16[4,384,192]{1,2,0:T(8,128)(2,1)S(1)}, bf16[4,384,192]{1,2,0:T(8,128)(2,1)}, u32[]{:S(2)}, u32[]{:S(2)}) collective-permute-start(bf16[4,384,192]{1,2,0:T(8,128)(2,1)S(1)} %all_gather.60), channel_id=1, source_target_pairs={{0,4},{4,0},{1,5},{5,1},{2,6},{6,2},{3,7},{7,3},{8,12},{12,8},{9,1... | collective-permute-start | bytes 1769480 | tf_op jit(solution)/shard_map/ppermute | solution.py:41
  131.5 50.8 %collective-permute-start.6 = (bf16[4,1,192,768]{3,2,1,0:T(8,128)(2,1)}, bf16[4,1,192,768]{3,2,1,0:T(8,128)(2,1)}, u32[]{:S(2)}, u32[]{:S(2)}) collective-permute-start(bf16[4,1,192,768]{3,2,1,0:T(8,128)(2,1)} %maximum_bitcast_fusion), channel_id=1, source_target_pairs={{0,16},{8,24},{16,0},{24,8},{1,17},{9,25},{17,1},{25,9},{2,18},{10... | collective-permute-start | bytes 3538952 | tf_op jit(solution)/shard_map/ppermute | solution.py:41
  142.5 45.8 %collective-permute-start.1 = (bf16[384,3,384]{0,2,1:T(8,128)(2,1)}, bf16[384,3,384]{0,2,1:T(8,128)(2,1)}, u32[]{:S(2)}, u32[]{:S(2)}) collective-permute-start(bf16[384,3,384]{0,2,1:T(8,128)(2,1)} %collective-permute-done), channel_id=1, source_target_pairs={{0,8},{8,0},{16,24},{24,16},{1,9},{9,1},{17,25},{25,17},{2,10},{10... | collective-permute-start | bytes 2654216 | tf_op jit(solution)/shard_map/ppermute | solution.py:41
  152.2 55.4 %collective-permute-start.29 = (bf16[4,768,1,192]{1,3,2,0:T(8,128)(2,1)}, bf16[4,768,1,192]{1,3,2,0:T(8,128)(2,1)}, u32[]{:S(2)}, u32[]{:S(2)}) collective-permute-start(bf16[4,768,1,192]{1,3,2,0:T(8,128)(2,1)} %maximum_bitcast_fusion.4), channel_id=1, source_target_pairs={{0,16},{8,24},{16,0},{24,8},{1,17},{9,25},{17,1},{25,9},{2,18},{10... | collective-permute-start | bytes 3538952 | tf_op jit(solution)/shard_map/ppermute | solution.py:41
  155.7 76.0 %collective-permute-start.9 = (bf16[4,768,1,192]{1,3,2,0:T(8,128)(2,1)}, bf16[4,768,1,192]{1,3,2,0:T(8,128)(2,1)}, u32[]{:S(2)}, u32[]{:S(2)}) collective-permute-start(bf16[4,768,1,192]{1,3,2,0:T(8,128)(2,1)} %maximum_bitcast_fusion.1), channel_id=1, source_target_pairs={{0,16},{8,24},{16,0},{24,8},{1,17},{9,25},{17,1},{25,9},{2,18},{10... | collective-permute-start | bytes 3538952 | tf_op jit(solution)/shard_map/ppermute | solution.py:41
  157.0 80.8 %collective-permute-start.12 = (bf16[384,2,384]{0,2,1:T(8,128)(2,1)}, bf16[384,2,384]{0,2,1:T(8,128)(2,1)}, u32[]{:S(2)}, u32[]{:S(2)}) collective-permute-start(bf16[384,2,384]{0,2,1:T(8,128)(2,1)} %collective-permute-done.11), channel_id=1, source_target_pairs={{0,8},{8,0},{16,24},{24,16},{1,9},{9,1},{17,25},{25,17},{2,10},{10... | collective-permute-start | bytes 1769480 | tf_op jit(solution)/shard_map/ppermute | solution.py:41
  188.3 106.9 %collective-permute-start.7 = (bf16[1536,768]{1,0:T(8,128)(2,1)}, bf16[1536,768]{1,0:T(8,128)(2,1)}, u32[]{:S(2)}, u32[]{:S(2)}) collective-permute-start(bf16[1536,768]{1,0:T(8,128)(2,1)} %bitcast.7), channel_id=1, source_target_pairs={{0,8},{8,0},{16,24},{24,16},{1,9},{9,1},{17,25},{25,17},{2,10},{10... | collective-permute-start | bytes 7077896 | tf_op jit(solution)/shard_map/ppermute | solution.py:41
  193.5 53.7 %collective-permute-start.2 = (bf16[2,640,384]{2,1,0:T(8,128)(2,1)S(1)}, bf16[2,640,384]{2,1,0:T(8,128)(2,1)S(1)}, u32[]{:S(2)}, u32[]{:S(2)}) collective-permute-start(bf16[2,640,384]{2,1,0:T(8,128)(2,1)S(1)} %slice.396), channel_id=1, source_target_pairs={{0,4},{4,8},{8,12},{12,16},{16,20},{20,24},{24,28},{1,5},{5,9},{9,... | collective-permute-start | bytes 2949128 | tf_op jit(solution)/shard_map/ppermute | solution.py:36
  207.6 39.6 %collective-permute-start.3 = (bf16[2,640,384]{2,1,0:T(8,128)(2,1)S(1)}, bf16[2,640,384]{2,1,0:T(8,128)(2,1)S(1)}, u32[]{:S(2)}, u32[]{:S(2)}) collective-permute-start(bf16[2,640,384]{2,1,0:T(8,128)(2,1)S(1)} %slice.396), channel_id=1, source_target_pairs={{0,8},{4,12},{8,16},{12,20},{16,24},{20,28},{1,9},{5,13},{9,17},{1... | collective-permute-start | bytes 2949128 | tf_op jit(solution)/shard_map/ppermute | solution.py:36
  237.8 61.4 %collective-permute-start.10 = (bf16[768,1536]{0,1:T(8,128)(2,1)}, bf16[768,1536]{0,1:T(8,128)(2,1)}, u32[]{:S(2)}, u32[]{:S(2)}) collective-permute-start(bf16[768,1536]{0,1:T(8,128)(2,1)} %bitcast.13), channel_id=1, source_target_pairs={{0,8},{8,0},{16,24},{24,16},{1,9},{9,1},{17,25},{25,17},{2,10},{10... | collective-permute-start | bytes 7077896 | tf_op jit(solution)/shard_map/ppermute | solution.py:41
  245.3 63.6 %collective-permute-start.15 = (bf16[1536,768]{1,0:T(8,128)(2,1)}, bf16[1536,768]{1,0:T(8,128)(2,1)}, u32[]{:S(2)}, u32[]{:S(2)}) collective-permute-start(bf16[1536,768]{1,0:T(8,128)(2,1)} %bitcast.24), channel_id=1, source_target_pairs={{0,8},{8,0},{16,24},{24,16},{1,9},{9,1},{17,25},{25,17},{2,10},{10... | collective-permute-start | bytes 7077896 | tf_op jit(solution)/shard_map/ppermute | solution.py:41
  264.5 110.0 %all-gather.9.cloned.1.call-start = ((), (), s32[]{:S(2)}) async-start(), calls=%async_computation.19 | async-start | bytes 2457600 | tf_op jit(solution)/shard_map/all_gather | solution.py:359
  314.2 116.2 %reduce-scatter.19.cloned.1.call-start = ((), (), s32[]{:S(2)}) async-start(), calls=%async_computation.20 | async-start | bytes 2457600 | tf_op jit(solution)/shard_map/reduce_scatter | solution.py:362
  330.7 43.8 %collective-permute-start.18 = (bf16[1536,384]{1,0:T(8,128)(2,1)S(1)}, bf16[1536,384]{1,0:T(8,128)(2,1)}, u32[]{:S(2)}, u32[]{:S(2)}) collective-permute-start(bf16[1536,384]{1,0:T(8,128)(2,1)S(1)} %get-tuple-element.169), channel_id=1, source_target_pairs={{0,4},{4,0},{1,5},{5,1},{2,6},{6,2},{3,7},{7,3},{8,12},{12,8},{9,1... | collective-permute-start | bytes 3538952 | tf_op jit(solution)/shard_map/ppermute | solution.py:41
  388.6 146.0 %all-gather.11.cloned.1.call-start = ((), (), s32[]{:S(2)}) async-start(), calls=%async_computation.21 | async-start | bytes 2457600 | tf_op jit(solution)/shard_map/all_gather | solution.py:359
  480.8 40.4 %collective-permute-start.26 = (bf16[4,1,192,768]{3,2,1,0:T(8,128)(2,1)}, bf16[4,1,192,768]{3,2,1,0:T(8,128)(2,1)}, u32[]{:S(2)}, u32[]{:S(2)}) collective-permute-start(bf16[4,1,192,768]{3,2,1,0:T(8,128)(2,1)} %maximum_bitcast_fusion.3), channel_id=1, source_target_pairs={{0,16},{8,24},{16,0},{24,8},{1,17},{9,25},{17,1},{25,9},{2,18},{10... | collective-permute-start | bytes 3538952 | tf_op jit(solution)/shard_map/ppermute | solution.py:41
  490.0 38.7 %collective-permute-start.34 = (bf16[4,1,192,768]{3,2,1,0:T(8,128)(2,1)}, bf16[4,1,192,768]{3,2,1,0:T(8,128)(2,1)}, u32[]{:S(2)}, u32[]{:S(2)}) collective-permute-start(bf16[4,1,192,768]{3,2,1,0:T(8,128)(2,1)} %maximum_bitcast_fusion.5), channel_id=1, source_target_pairs={{0,16},{8,24},{16,0},{24,8},{1,17},{9,25},{17,1},{25,9},{2,18},{10... | collective-permute-start | bytes 3538952 | tf_op jit(solution)/shard_map/ppermute | solution.py:41
  534.6 88.7 %collective-permute-start.27 = (bf16[1536,768]{1,0:T(8,128)(2,1)}, bf16[1536,768]{1,0:T(8,128)(2,1)}, u32[]{:S(2)}, u32[]{:S(2)}) collective-permute-start(bf16[1536,768]{1,0:T(8,128)(2,1)} %bitcast.36), channel_id=1, source_target_pairs={{0,8},{8,0},{16,24},{24,16},{1,9},{9,1},{17,25},{25,17},{2,10},{10... | collective-permute-start | bytes 7077896 | tf_op jit(solution)/shard_map/ppermute | solution.py:41
  556.8 70.4 %collective-permute-start.30 = (bf16[768,1536]{0,1:T(8,128)(2,1)}, bf16[768,1536]{0,1:T(8,128)(2,1)}, u32[]{:S(2)}, u32[]{:S(2)}) collective-permute-start(bf16[768,1536]{0,1:T(8,128)(2,1)} %bitcast.40), channel_id=1, source_target_pairs={{0,8},{8,0},{16,24},{24,16},{1,9},{9,1},{17,25},{25,17},{2,10},{10... | collective-permute-start | bytes 7077896 | tf_op jit(solution)/shard_map/ppermute | solution.py:41
  570.0 67.0 %collective-permute-start.35 = (bf16[1536,768]{1,0:T(8,128)(2,1)}, bf16[1536,768]{1,0:T(8,128)(2,1)}, u32[]{:S(2)}, u32[]{:S(2)}) collective-permute-start(bf16[1536,768]{1,0:T(8,128)(2,1)} %bitcast.49), channel_id=1, source_target_pairs={{0,8},{8,0},{16,24},{24,16},{1,9},{9,1},{17,25},{25,17},{2,10},{10... | collective-permute-start | bytes 7077896 | tf_op jit(solution)/shard_map/ppermute | solution.py:41
  592.5 106.9 %all-gather.13.cloned.1.call-start = ((), (), s32[]{:S(2)}) async-start(), calls=%async_computation.22 | async-start | bytes 2457600 | tf_op jit(solution)/shard_map/all_gather | solution.py:359
  642.6 94.0 %all-gather.15.cloned.1.call-start = ((), (), s32[]{:S(2)}) async-start(), calls=%async_computation.24 | async-start | bytes 2457600 | tf_op jit(solution)/shard_map/all_gather | solution.py:359
  651.4 188.3 %reduce-scatter.23.cloned.1.call-start = ((), (), s32[]{:S(2)}) async-start(), calls=%async_computation.25 | async-start | bytes 2457600 | tf_op jit(solution)/shard_map/reduce_scatter | solution.py:362
  655.8 43.6 %collective-permute-start.38 = (bf16[1536,384]{1,0:T(8,128)(2,1)S(1)}, bf16[1536,384]{1,0:T(8,128)(2,1)}, u32[]{:S(2)}, u32[]{:S(2)}) collective-permute-start(bf16[1536,384]{1,0:T(8,128)(2,1)S(1)} %get-tuple-element.157), channel_id=1, source_target_pairs={{0,4},{4,0},{1,5},{5,1},{2,6},{6,2},{3,7},{7,3},{8,12},{12,8},{9,1... | collective-permute-start | bytes 3538952 | tf_op jit(solution)/shard_map/ppermute | solution.py:41
  752.5 108.1 %reduce-scatter.21.cloned.1.call-start = ((), (), s32[]{:S(2)}) async-start(), calls=%async_computation.23 | async-start | bytes 2457600 | tf_op jit(solution)/shard_map/reduce_scatter | solution.py:362
  789.3 47.7 %collective-permute-start.102 = (bf16[384,1536]{1,0:T(8,128)(2,1)}, bf16[384,1536]{1,0:T(8,128)(2,1)}, u32[]{:S(2)}, u32[]{:S(2)}) collective-permute-start(bf16[384,1536]{1,0:T(8,128)(2,1)} %slice.463), channel_id=1, source_target_pairs={{0,4},{4,0},{1,5},{5,1},{2,6},{6,2},{3,7},{7,3},{8,12},{12,8},{9,1... | collective-permute-start | bytes 3538952 | tf_op jit(solution)/shard_map/ppermute | solution.py:41
  815.9 122.6 %collective-permute-start.111 = (bf16[1536,384]{0,1:T(8,128)(2,1)}, bf16[1536,384]{0,1:T(8,128)(2,1)}, u32[]{:S(2)}, u32[]{:S(2)}) collective-permute-start(bf16[1536,384]{0,1:T(8,128)(2,1)} %add_convert_fusion.13), channel_id=1, source_target_pairs={{0,16},{8,24},{16,0},{24,8},{1,17},{9,25},{17,1},{25,9},{2,18},{10... | collective-permute-start | bytes 3538952 | tf_op jit(solution)/shard_map/ppermute | solution.py:41
  872.1 109.2 %reduce-scatter.43.cloned.1.call-start = ((), (), s32[]{:S(2)}) async-start(), calls=%async_computation.37 | async-start | bytes 983040
  876.6 85.3 %collective-permute-start.92 = (bf16[1536,768]{1,0:T(8,128)(2,1)}, bf16[1536,768]{1,0:T(8,128)(2,1)}, u32[]{:S(2)}, u32[]{:S(2)}) collective-permute-start(bf16[1536,768]{1,0:T(8,128)(2,1)} %slice.453), channel_id=1, source_target_pairs={{0,8},{8,0},{16,24},{24,16},{1,9},{9,1},{17,25},{25,17},{2,10},{10... | collective-permute-start | bytes 7077896 | tf_op jit(solution)/shard_map/ppermute | solution.py:41
  926.9 143.1 %reduce-scatter.25.cloned.1.call-start = ((), (), s32[]{:S(2)}) async-start(), calls=%async_computation.26 | async-start | bytes 2457600 | tf_op jit(solution)/shard_map/reduce_scatter | solution.py:362
  930.2 52.9 %collective-permute-start.74 = (bf16[768,1536]{0,1:T(8,128)(2,1)}, bf16[768,1536]{0,1:T(8,128)(2,1)}, u32[]{:S(2)}, u32[]{:S(2)}) collective-permute-start(bf16[768,1536]{0,1:T(8,128)(2,1)} %slice.437), channel_id=1, source_target_pairs={{0,8},{8,0},{16,24},{24,16},{1,9},{9,1},{17,25},{25,17},{2,10},{10... | collective-permute-start | bytes 7077896 | tf_op jit(solution)/shard_map/ppermute | solution.py:41
  952.8 46.0 %collective-permute-start.64 = (bf16[1536,768]{1,0:T(8,128)(2,1)}, bf16[1536,768]{1,0:T(8,128)(2,1)}, u32[]{:S(2)}, u32[]{:S(2)}) collective-permute-start(bf16[1536,768]{1,0:T(8,128)(2,1)} %slice.429), channel_id=1, source_target_pairs={{0,8},{8,0},{16,24},{24,16},{1,9},{9,1},{17,25},{25,17},{2,10},{10... | collective-permute-start | bytes 7077896 | tf_op jit(solution)/shard_map/ppermute | solution.py:41
  952.8 132.1 %collective-permute-start.112 = (bf16[1536,384]{0,1:T(8,128)(2,1)}, bf16[1536,384]{0,1:T(8,128)(2,1)}, u32[]{:S(2)}, u32[]{:S(2)}) collective-permute-start(bf16[1536,384]{0,1:T(8,128)(2,1)} %add_convert_fusion.12), channel_id=1, source_target_pairs={{0,8},{8,0},{16,24},{24,16},{1,9},{9,1},{17,25},{25,17},{2,10},{10... | collective-permute-start | bytes 3538952 | tf_op jit(solution)/shard_map/ppermute | solution.py:41
  961.9 160.1 %reduce-scatter.41.cloned.1.call-start = ((), (), s32[]{:S(2)}) async-start(), calls=%async_computation.36 | async-start | bytes 737280 | tf_op jit(solution)/shard_map/reduce_scatter | solution.py:422
  981.3 119.9 %collective-permute-start.104 = (bf16[384,1536]{1,0:T(8,128)(2,1)}, bf16[384,1536]{1,0:T(8,128)(2,1)}, u32[]{:S(2)}, u32[]{:S(2)}) collective-permute-start(bf16[384,1536]{1,0:T(8,128)(2,1)} %add_convert_fusion.16), channel_id=1, source_target_pairs={{0,8},{8,0},{16,24},{24,16},{1,9},{9,1},{17,25},{25,17},{2,10},{10... | collective-permute-start | bytes 3538952 | tf_op jit(solution)/shard_map/ppermute | solution.py:41
  1002.9 42.1 %collective-permute-start.65 = (bf16[1536,384]{1,0:T(8,128)(2,1)}, bf16[1536,384]{1,0:T(8,128)(2,1)}, u32[]{:S(2)}, u32[]{:S(2)}) collective-permute-start(bf16[1536,384]{1,0:T(8,128)(2,1)} %slice.431), channel_id=1, source_target_pairs={{0,4},{4,0},{1,5},{5,1},{2,6},{6,2},{3,7},{7,3},{8,12},{12,8},{9,1... | collective-permute-start | bytes 3538952 | tf_op jit(solution)/shard_map/ppermute | solution.py:41
  1022.7 100.0 %reduce-scatter.37.cloned.1.call-start = ((), (), s32[]{:S(2)}) async-start(), calls=%async_computation.34 | async-start | bytes 983040 | tf_op jit(solution)/shard_map/reduce_scatter | solution.py:422
  1053.5 70.5 %reduce-scatter.33.cloned.1.call-start = ((), (), s32[]{:S(2)}) async-start(), calls=%async_computation.32 | async-start | bytes 737280 | tf_op jit(solution)/shard_map/reduce_scatter | solution.py:422
  1070.0 77.1 %all-gather.17.cloned.1.call-start = ((), (), s32[]{:S(2)}) async-start(), calls=%async_computation.27 | async-start | bytes 2457600 | tf_op jit(solution)/shard_map/all_gather | solution.py:359
  1074.3 128.4 %reduce-scatter.27.cloned.1.call-start = ((), (), s32[]{:S(2)}) async-start(), calls=%async_computation.28 | async-start | bytes 2457600 | tf_op jit(solution)/shard_map/reduce_scatter | solution.py:362
  1122.0 292.4 %collective-permute-start.58 = (bf16[384,3,384]{2,0,1:T(8,128)(2,1)}, bf16[384,3,384]{2,0,1:T(8,128)(2,1)}, u32[]{:S(2)}, u32[]{:S(2)}) collective-permute-start(bf16[384,3,384]{2,0,1:T(8,128)(2,1)} %add_convert_fusion.30), channel_id=1, source_target_pairs={{0,8},{8,0},{16,24},{24,16},{1,9},{9,1},{17,25},{25,17},{2,10},{10... | collective-permute-start | bytes 2654216 | tf_op jit(solution)/shard_map/ppermute | solution.py:41
  1122.0 54.1 %collective-permute-start.95 = (bf16[192,384]{1,0:T(8,128)(2,1)}, bf16[192,384]{1,0:T(8,128)(2,1)S(1)}, u32[]{:S(2)}, u32[]{:S(2)}) collective-permute-start(bf16[192,384]{1,0:T(8,128)(2,1)} %bitcast.362), channel_id=1, source_target_pairs={{0,16},{8,24},{16,0},{24,8},{1,17},{9,25},{17,1},{25,9},{2,18},{10... | collective-permute-start | bytes 442376 | tf_op jit(solution)/shard_map/ppermute | solution.py:41
  1122.6 54.3 %collective-permute-start.77 = (bf16[384,192]{1,0:T(8,128)(2,1)}, bf16[384,192]{1,0:T(8,128)(2,1)S(1)}, u32[]{:S(2)}, u32[]{:S(2)}) collective-permute-start(bf16[384,192]{1,0:T(8,128)(2,1)} %bitcast.359), channel_id=1, source_target_pairs={{0,16},{8,24},{16,0},{24,8},{1,17},{9,25},{17,1},{25,9},{2,18},{10... | collective-permute-start | bytes 442376 | tf_op jit(solution)/shard_map/ppermute | solution.py:41
  1124.0 53.9 %collective-permute-start.67 = (bf16[192,384]{1,0:T(8,128)(2,1)}, bf16[192,384]{1,0:T(8,128)(2,1)S(1)}, u32[]{:S(2)}, u32[]{:S(2)}) collective-permute-start(bf16[192,384]{1,0:T(8,128)(2,1)} %bitcast.363), channel_id=1, source_target_pairs={{0,16},{8,24},{16,0},{24,8},{1,17},{9,25},{17,1},{25,9},{2,18},{10... | collective-permute-start | bytes 442376 | tf_op jit(solution)/shard_map/ppermute | solution.py:41
  1162.3 294.5 %reduce-scatter.45.cloned.1.call-start = ((), (), s32[]{:S(2)}) async-start(), calls=%async_computation.38 | async-start | bytes 983040
  1183.9 185.6 %collective-permute-start.106 = (bf16[1536,384]{0,1:T(8,128)(2,1)}, bf16[1536,384]{0,1:T(8,128)(2,1)}, u32[]{:S(2)}, u32[]{:S(2)}) collective-permute-start(bf16[1536,384]{0,1:T(8,128)(2,1)} %slice.467), channel_id=1, source_target_pairs={{0,4},{4,0},{1,5},{5,1},{2,6},{6,2},{3,7},{7,3},{8,12},{12,8},{9,1... | collective-permute-start | bytes 3538952 | tf_op jit(solution)/shard_map/ppermute | solution.py:41
  1242.3 38.6 %collective-permute-start.59 = (bf16[1536,768]{1,0:T(8,128)(2,1)}, bf16[1536,768]{1,0:T(8,128)(2,1)}, u32[]{:S(2)}, u32[]{:S(2)}) collective-permute-start(bf16[1536,768]{1,0:T(8,128)(2,1)} %slice.425), channel_id=1, source_target_pairs={{0,8},{8,0},{16,24},{24,16},{1,9},{9,1},{17,25},{25,17},{2,10},{10... | collective-permute-start | bytes 7077896 | tf_op jit(solution)/shard_map/ppermute | solution.py:41
  1259.3 272.7 %reduce-scatter.39.cloned.1.call-start = ((), (), s32[]{:S(2)}) async-start(), calls=%async_computation.35 | async-start | bytes 737280 | tf_op jit(solution)/shard_map/reduce_scatter | solution.py:422
  1263.5 38.7 %collective-permute-start.70 = (bf16[384,1536]{0,1:T(8,128)(2,1)}, bf16[384,1536]{0,1:T(8,128)(2,1)}, u32[]{:S(2)}, u32[]{:S(2)}) collective-permute-start(bf16[384,1536]{0,1:T(8,128)(2,1)} %slice.435), channel_id=1, source_target_pairs={{0,4},{4,0},{1,5},{5,1},{2,6},{6,2},{3,7},{7,3},{8,12},{12,8},{9,1... | collective-permute-start | bytes 3538952 | tf_op jit(solution)/shard_map/ppermute | solution.py:41
  1285.7 41.7 %collective-permute-start.60 = (bf16[1536,384]{1,0:T(8,128)(2,1)}, bf16[1536,384]{1,0:T(8,128)(2,1)}, u32[]{:S(2)}, u32[]{:S(2)}) collective-permute-start(bf16[1536,384]{1,0:T(8,128)(2,1)} %slice.427), channel_id=1, source_target_pairs={{0,4},{4,0},{1,5},{5,1},{2,6},{6,2},{3,7},{7,3},{8,12},{12,8},{9,1... | collective-permute-start | bytes 3538952 | tf_op jit(solution)/shard_map/ppermute | solution.py:41
  1293.2 85.4 %collective-permute-start.98 = (bf16[384,1536]{1,0:T(8,128)(2,1)}, bf16[384,1536]{1,0:T(8,128)(2,1)}, u32[]{:S(2)}, u32[]{:S(2)}) collective-permute-start(bf16[384,1536]{1,0:T(8,128)(2,1)} %slice.459), channel_id=1, source_target_pairs={{0,4},{4,0},{1,5},{5,1},{2,6},{6,2},{3,7},{7,3},{8,12},{12,8},{9,1... | collective-permute-start | bytes 3538952 | tf_op jit(solution)/shard_map/ppermute | solution.py:41
  1296.9 246.2 %reduce-scatter.35.cloned.1.call-start = ((), (), s32[]{:S(2)}) async-start(), calls=%async_computation.33 | async-start | bytes 983040 | tf_op jit(solution)/shard_map/reduce_scatter | solution.py:422
  1330.9 42.7 %collective-permute-start.61 = (bf16[4,1,192,384]{3,2,1,0:T(8,128)(2,1)}, bf16[4,1,192,384]{3,2,1,0:T(8,128)(2,1)}, u32[]{:S(2)}, u32[]{:S(2)}) collective-permute-start(bf16[4,1,192,384]{3,2,1,0:T(8,128)(2,1)} %constant_dynamic-slice_fusion.7), channel_id=1, source_target_pairs={{0,16},{8,24},{16,0},{24,8},{1,17},{9,25},{17,1},{25,9},{2,18},{10... | collective-permute-start | bytes 1769480 | tf_op jit(solution)/shard_map/ppermute | solution.py:41
  1337.1 206.2 %reduce-scatter.31.cloned.1.call-start = ((), (), s32[]{:S(2)}) async-start(), calls=%async_computation.31 | async-start | bytes 737280 | tf_op jit(solution)/shard_map/reduce_scatter | solution.py:422
  1378.5 176.1 %reduce-scatter.29.cloned.1.call-start = ((), (), s32[]{:S(2)}) async-start(), calls=%async_computation.29 | async-start | bytes 2457600 | tf_op jit(solution)/shard_map/reduce_scatter | solution.py:362
  1401.7 52.6 %collective-permute-start.99 = (bf16[384,1536]{1,0:T(8,128)(2,1)}, bf16[384,1536]{1,0:T(8,128)(2,1)S(1)}, u32[]{:S(2)}, u32[]{:S(2)}) collective-permute-start(bf16[384,1536]{1,0:T(8,128)(2,1)} %add_convert_fusion.19), channel_id=1, source_target_pairs={{0,16},{8,24},{16,0},{24,8},{1,17},{9,25},{17,1},{25,9},{2,18},{10... | collective-permute-start | bytes 3538952 | tf_op jit(solution)/shard_map/ppermute | solution.py:41
  1410.4 194.7 %all-reduce.4.cloned.1.call-start = ((), (), s32[]{:S(2)}) async-start(), calls=%async_computation.30 | async-start | bytes 3145728 | tf_op jit(solution)/shard_map/psum | solution.py:586
  1432.4 40.2 %collective-permute-start.108 = (bf16[1536,384]{0,1:T(8,128)(2,1)}, bf16[1536,384]{0,1:T(8,128)(2,1)}, u32[]{:S(2)}, u32[]{:S(2)}) collective-permute-start(bf16[1536,384]{0,1:T(8,128)(2,1)} %add_convert_fusion.14), channel_id=1, source_target_pairs={{0,8},{8,0},{16,24},{24,16},{1,9},{9,1},{17,25},{25,17},{2,10},{10... | collective-permute-start | bytes 3538952 | tf_op jit(solution)/shard_map/ppermute | solution.py:41
  1456.8 42.2 %collective-permute-start.100 = (bf16[384,1536]{1,0:T(8,128)(2,1)}, bf16[384,1536]{1,0:T(8,128)(2,1)}, u32[]{:S(2)}, u32[]{:S(2)}) collective-permute-start(bf16[384,1536]{1,0:T(8,128)(2,1)} %add_convert_fusion.18), channel_id=1, source_target_pairs={{0,8},{8,0},{16,24},{24,16},{1,9},{9,1},{17,25},{25,17},{2,10},{10... | collective-permute-start | bytes 3538952 | tf_op jit(solution)/shard_map/ppermute | solution.py:41
  1543.0 38.5 %collective-permute-start.54 = (bf16[384,3,384]{2,0,1:T(8,128)(2,1)S(1)}, bf16[384,3,384]{2,0,1:T(8,128)(2,1)}, u32[]{:S(2)}, u32[]{:S(2)}) collective-permute-start(bf16[384,3,384]{2,0,1:T(8,128)(2,1)S(1)} %add_convert_fusion.32), channel_id=1, source_target_pairs={{0,8},{8,0},{16,24},{24,16},{1,9},{9,1},{17,25},{25,17},{2,10},{10... | collective-permute-start | bytes 2654216 | tf_op jit(solution)/shard_map/ppermute | solution.py:41
  (307 other events, 5425.6 us)
Sparse Core Ops, SparseCore 0:
  79.0 55.9 all-gather.6
  314.3 51.0 all-gather.8
  388.7 41.6 reduce-scatter.18
  433.4 55.6 all-gather.10
  642.7 49.4 all-gather.12
  694.2 42.3 all-gather.14
  752.6 40.2 reduce-scatter.22
  795.8 40.6 reduce-scatter.20
  927.0 27.0 reduce-scatter.42
  962.0 44.2 reduce-scatter.24
  1022.8 24.8 reduce-scatter.40
  1053.6 26.0 reduce-scatter.36
  1082.6 21.1 reduce-scatter.32
  1105.2 41.8 all-gather.16
  1162.5 40.2 reduce-scatter.26
  1251.0 28.8 reduce-scatter.44
  1297.0 20.2 reduce-scatter.38
  1337.2 21.7 reduce-scatter.34
  1378.6 20.8 reduce-scatter.30
  1410.5 41.5 reduce-scatter.28
  1472.8 132.3 all-reduce.3
